TPU v7x, 32 devices: a whole 2x2x4 slice. The times are simulated.
32 devices in a mesh: case: 2 (over x), tile: 16 (over z, y, core).
Axes of the slice: x: 2, y: 2, z: 4, core: 2. Of those that a mesh axis runs over, the one named last changes fastest.
Arguments:
- segment_maps: bfloat16 [128, 256, 256], P(('case', 'tile')), parts along dimension 0, may hold values from -1.5 to 1.5
- cotangent: bfloat16 [768, 64, 64], P(('case', 'tile')), parts along dimension 0, may hold values from -6 to 6
- wavelengths: float32 [16], replicated, may hold values from 0.8 to 1.6
- intersections: int32 [512, 2, 5], P(('case', 'tile')), parts along dimension 0, may hold values from 0 to 192, as said below
Outputs:
- grad_maps: float32 [128, 256, 256], P(('case', 'tile')), parts along dimension 0
There are 2 independent parts, one for each index of `case`. A program takes and returns all parts, laid end to end along the dimension named above; an argument that names none is the same for every part. Nothing has to cross between parts.
Inputs may be any that keep to these rules, and one draw needn't show every extreme that they name: `intersections`: column 0 is 0 or 1; column 1 is below 4, column 2 below 24, columns 3 and 4 at most 192. In every draw one tile receives 2 live slots from every segment owner.
All inputs are finite; a program needn't handle non-finite values.
Results may differ from a plain program's by a relative error of at most 0.0046.
Values may be sent and summed in bfloat16 or wider, within the bound.
No kernel may reach another device: no remote copies, remote signals or barrier semaphores. Data moves between devices by JAX's collectives and lax.ppermute only.
A program may use at most 64 MiB of HBM per device.

v0:
```python
import math

import jax
import jax.numpy as jnp
from jax import lax
from jax.sharding import PartitionSpec as P

SUB = 64


SAMPLING = 0.5
TWO_PI = 2.0 * math.pi


def hex_mask(extent):
    across = jnp.abs(2 * jnp.arange(extent, dtype=jnp.int32) - (extent - 1))
    down = across[:, None]
    sideways = across[None, :]
    inside = (8 * down <= 7 * (extent - 1)) & (7 * sideways + 4 * down <= 7 * (extent - 1))
    return inside.astype(jnp.bfloat16)


def lens_tables(wavelength, focal, pupil):
    focal_pos = jnp.arange(focal, dtype=jnp.int32) - focal // 2
    pupil_pos = jnp.arange(pupil, dtype=jnp.int32) - pupil // 2
    product = (focal_pos[:, None] * pupil_pos[None, :]).astype(jnp.float32)
    angles = product * (-TWO_PI * SAMPLING / pupil) / wavelength
    return (jnp.cos(angles).astype(jnp.bfloat16), jnp.sin(angles).astype(jnp.bfloat16))


def mix(form, first, second):
    return jnp.einsum(form, first, second, preferred_element_type=jnp.float32)


def on_device(segment_maps, cotangent, wavelengths, intersections):
    peers = intersections.shape[0]
    per_peer = intersections.shape[1]
    slots = peers * per_peer
    pupil = SUB
    focal = cotangent.shape[1]
    area = pupil * pupil
    waves = wavelengths.shape[0]
    lens_count = cotangent.shape[0]
    seg_count = segment_maps.shape[0]
    seg_width = segment_maps.shape[1]
    entries = intersections.reshape(slots, 5)
    mask = hex_mask(seg_width)

    def shade_at(row_off, col_off, keep):
        return lax.dynamic_slice(mask, (row_off, col_off), (pupil, pupil)) * keep.astype(
            jnp.bfloat16
        )

    def cutout(segment_id, row_off, col_off, keep):
        piece = lax.dynamic_slice(segment_maps, (segment_id, row_off, col_off), (1, pupil, pupil))[
            0
        ]
        return piece * shade_at(row_off, col_off, keep)

    patches = jax.vmap(cutout)(entries[:, 1], entries[:, 3], entries[:, 4], entries[:, 0])
    outgoing = patches.reshape(peers, per_peer, area)
    arriving, arriving_table = (
        lax.all_to_all(outgoing, "tile", split_axis=0, concat_axis=0, tiled=True),
        lax.all_to_all(intersections, "tile", split_axis=0, concat_axis=0, tiled=True),
    )
    table = arriving_table.reshape(slots, 5)
    arriving_shades = jax.vmap(shade_at)(table[:, 3], table[:, 4], table[:, 0]).reshape(slots, area)
    selector = (
        (table[:, 2][None, :] == jnp.arange(lens_count, dtype=jnp.int32)[:, None])
        & (table[:, 0][None, :] == 1)
    ).astype(jnp.bfloat16)
    opd = jnp.dot(
        selector, arriving.reshape(slots, area), preferred_element_type=jnp.float32
    ).reshape(lens_count, pupil, pupil)
    amplitude = jnp.dot(selector, arriving_shades, preferred_element_type=jnp.float32).reshape(
        lens_count, pupil, pupil
    )
    weight = cotangent.astype(jnp.float32) * (2.0 / waves)

    def one_wave(wave_idx, totals):
        wavelength = wavelengths[wave_idx]
        real_tab, imag_tab = lens_tables(wavelength, focal, pupil)
        phase = TWO_PI / wavelength * opd
        cosine = jnp.cos(phase)
        sine = jnp.sin(phase)
        field_re = (amplitude * cosine).astype(jnp.bfloat16)
        field_im = (amplitude * sine).astype(jnp.bfloat16)
        left_re = (
            mix("ux,lxy->luy", real_tab, field_re) - mix("ux,lxy->luy", imag_tab, field_im)
        ).astype(jnp.bfloat16)
        left_im = (
            mix("ux,lxy->luy", real_tab, field_im) + mix("ux,lxy->luy", imag_tab, field_re)
        ).astype(jnp.bfloat16)
        image_re = (
            mix("luy,vy->luv", left_re, real_tab) - mix("luy,vy->luv", left_im, imag_tab)
        ) / pupil
        image_im = (
            mix("luy,vy->luv", left_re, imag_tab) + mix("luy,vy->luv", left_im, real_tab)
        ) / pupil
        hold_re = (weight * image_re).astype(jnp.bfloat16)
        hold_im = (weight * image_im).astype(jnp.bfloat16)
        back_re = (
            mix("ux,luv->lxv", real_tab, hold_re) + mix("ux,luv->lxv", imag_tab, hold_im)
        ).astype(jnp.bfloat16)
        back_im = (
            mix("ux,luv->lxv", real_tab, hold_im) - mix("ux,luv->lxv", imag_tab, hold_re)
        ).astype(jnp.bfloat16)
        grad_re = (
            mix("lxv,vy->lxy", back_re, real_tab) + mix("lxv,vy->lxy", back_im, imag_tab)
        ) / pupil
        grad_im = (
            mix("lxv,vy->lxy", back_im, real_tab) - mix("lxv,vy->lxy", back_re, imag_tab)
        ) / pupil
        return totals + TWO_PI / wavelength * amplitude * (cosine * grad_im - sine * grad_re)

    grad_opd = lax.fori_loop(0, waves, one_wave, jnp.zeros((lens_count, pupil, pupil), jnp.float32))
    picked = jnp.dot(
        selector.astype(jnp.float32).T,
        grad_opd.reshape(lens_count, area),
        preferred_element_type=jnp.float32,
        precision=lax.Precision.HIGHEST,
    )
    grad_patches = (picked * arriving_shades.astype(jnp.float32)).astype(jnp.bfloat16)
    returned = lax.all_to_all(
        grad_patches.reshape(peers, per_peer, area), "tile", split_axis=0, concat_axis=0, tiled=True
    )
    returned = returned.reshape(slots, pupil, pupil)
    offsets = jnp.arange(pupil, dtype=jnp.int32)
    columns_all = jnp.arange(seg_width, dtype=jnp.int32)
    col_hot = (
        entries[:, 4][:, None, None] + offsets[None, :, None] == columns_all[None, None, :]
    ).astype(jnp.bfloat16)
    placed = (
        mix("kij,kjc->kic", returned, col_hot)
        .astype(jnp.bfloat16)
        .reshape(slots * pupil, seg_width)
    )
    row_target = (entries[:, 3][:, None] + offsets[None, :]).reshape(slots * pupil)
    seg_owner = jnp.broadcast_to(entries[:, 1][:, None], (slots, pupil)).reshape(slots * pupil)

    def one_segment(seg_index):
        row_hot = (
            (row_target[None, :] == columns_all[:, None]) & (seg_owner[None, :] == seg_index)
        ).astype(jnp.bfloat16)
        return jnp.dot(row_hot, placed, preferred_element_type=jnp.float32)

    return lax.map(one_segment, jnp.arange(seg_count, dtype=jnp.int32))


def solution(mesh):
    return jax.shard_map(
        on_device,
        mesh=mesh,
        in_specs=(
            P(("case", "tile"), None, None),
            P(("case", "tile"), None, None),
            P(),
            P(("case", "tile"), None, None),
        ),
        out_specs=P(("case", "tile"), None, None),
        check_vma=False,
    )
```

profile of v0, /device:TPU:0, one launch (start us, length us, event | category | flops | bytes accessed | tf_op | source)
XLA Modules:
  0.0 753.0 jit_solution(1604905217732729590)
XLA Ops:
  1.4 7.4 all-to-all-start
  11.5 107.1 %while.31 = (s32[]{:T(128)}, bf16[4,256,256]{2,1,0:T(8,128)(2,1)}, s32[32,3]{0,1:T(4,128)S(1)}, bf16[32,1,64,64]{3,2,1,0:T(8,128)(2,1)S(1)}, s32[]{:T(128)}) while((s32[]{:T(128)}, bf16[4,256,256]{2,1,0:T(8,128)(2,1)}, s32[32,3]{0,1:T(4,128)S(1)}, bf16[32,1,64,64]{3,2,1,0:T(8,128)(2,1)S(1)}, s32[]{:T(128)}) %tuple.124), condition=%wide.while_cond.1, body=%wide.while_body.1.sunk | while | flops 2 | bytes 24705 | solution.py:55
  119.3 60.7 %while.32 = (s32[]{:T(128)}, bf16[256,256]{1,0:T(8,128)(2,1)S(1)}, s32[32,2]{0,1:T(2,128)S(1)}, bf16[32,64,64]{2,1,0:T(8,128)(2,1)S(1)}, s32[]{:T(128)}) while((s32[]{:T(128)}, bf16[256,256]{1,0:T(8,128)(2,1)S(1)}, s32[32,2]{0,1:T(2,128)S(1)}, bf16[32,64,64]{2,1,0:T(8,128)(2,1)S(1)}, s32[]{:T(128)}) %tuple.127), condition=%wide.while_cond.2, body=%wide.while_body.2.sunk | while | flops 2 | bytes 32877 | solution.py:50
  181.7 6.0 all-to-all-start.1
  188.3 61.6 %while.30 = (s32[]{:T(128)}, bf16[256,256]{1,0:T(8,128)(2,1)S(1)}, s32[32,2]{0,1:T(2,128)S(1)}, bf16[32,64,64]{2,1,0:T(8,128)(2,1)S(1)}, s32[]{:T(128)}) while((s32[]{:T(128)}, bf16[256,256]{1,0:T(8,128)(2,1)S(1)}, s32[32,2]{0,1:T(2,128)S(1)}, bf16[32,64,64]{2,1,0:T(8,128)(2,1)S(1)}, s32[]{:T(128)}) %tuple.137), condition=%wide.while_cond, body=%wide.while_body.sunk | while | flops 2 | bytes 32877 | solution.py:50
  253.0 469.3 %while.34 = (s32[]{:T(128)}, f32[24,64,64]{2,1,0:T(8,128)}, f32[16]{0:T(128)}, f32[24,64,64]{2,1,0:T(8,128)S(1)}, f32[24,64,64]{2,1,0:T(8,128)S(1)}, /*index=5*/...) while((s32[]{:T(128)}, f32[24,64,64]{2,1,0:T(8,128)}, f32[16]{0:T(128)}, ...), condition=%wide.region_1.0_spmd.clone, body=%wide.region_0.0_spmd.clone.sunk | while | flops 204996672 | bytes 15339979 | solution.py:116
  272.3 4.3 fusion.280
  276.6 5.6 fusion.282
  301.5 4.3 fusion.280
  305.8 5.7 fusion.282
  330.8 4.3 fusion.280
  335.2 5.7 fusion.282
  364.5 5.7 fusion.282
  389.5 4.3 fusion.280
  393.8 5.7 fusion.282
  423.2 5.7 fusion.282
  452.5 5.7 fusion.282
  477.5 4.3 fusion.280
  481.9 5.7 fusion.282
  511.2 5.7 fusion.282
  536.2 4.3 fusion.280
  540.5 5.7 fusion.282
  565.6 4.3 fusion.280
  569.9 5.7 fusion.282
  599.2 5.7 fusion.282
  628.6 5.7 fusion.282
  657.9 5.7 fusion.282
  687.2 5.7 fusion.282
  716.6 5.7 fusion.282
  725.1 6.0 all-to-all-start.2
  731.2 10.0 %all-to-all-done.2 = bf16[16,2,4096]{2,1,0:T(2,128)(2,1)S(1)} async-done(((bf16[16,2,4096]{2,1,0:T(2,128)(2,1)}), bf16[16,2,4096]{2,1,0:T(2,128)(2,1)S(1)}, u32[]{:S(2)}, u32[]{:S(2)}) %all-to-all-start.2) | async-done | bytes 262176 | tf_op jit(solution)/shard_map/all_to_all | solution.py:124
  742.1 11.0 %while.33 = (s32[]{:T(128)}, f32[4,256,256]{2,1,0:T(8,128)}, s32[4]{0:T(128)S(1)}, bf16[2048,256]{1,0:T(8,128)(2,1)S(1)}, s32[32]{0:T(128)S(1)}, /*index=5*/s32[32]{0:T(128)S(1)}, s32[]{:T(128)}) while((s32[]{:T(128)}, f32[4,256,256]{2,1,0:T(8,128)}, s32[4]{0:T(128)S(1)}, bf16[2048,256]{1,0:T(8,128)(2,1)S(1)}, s32[32]{0:T(128)S(1)}, ...), condition=%wide.region_3.4_spmd.clone, body=%wide.region_2.3_spmd.clone.sunk | while | flops 269486112 | bytes 1352605 | solution.py:147
  (656 shorter events, 588.1 us)
Async XLA Ops:
  1.4 180.3 %all-to-all-start = ((s32[16,2,5]{2,1,0:T(2,128)}), s32[16,2,5]{2,1,0:T(2,128)S(1)}, u32[]{:S(2)}, u32[]{:S(2)}) async-start(s32[16,2,5]{2,1,0:T(2,128)} %copy.122), calls=%async_computation | async-start | bytes 32768 | tf_op jit(solution)/shard_map/all_to_all | solution.py:64
  119.2 62.3 %copy-start.2 = (bf16[24,64,64]{2,1,0:T(8,128)(2,1)S(1)}, bf16[24,64,64]{2,1,0:T(8,128)(2,1)}, u32[]{:S(2)}) copy-start(bf16[24,64,64]{2,1,0:T(8,128)(2,1)} %param.9) | copy-start | bytes 589828
  181.7 70.1 %all-to-all-start.1 = ((bf16[16,2,4096]{2,1,0:T(2,128)(2,1)}), bf16[16,2,4096]{2,1,0:T(2,128)(2,1)S(1)}, u32[]{:S(2)}, u32[]{:S(2)}) async-start(bf16[16,2,4096]{2,1,0:T(2,128)(2,1)} %multiply_multiply_fusion), calls=%async_computation.1 | async-start | bytes 524288 | tf_op jit(solution)/shard_map/all_to_all | solution.py:63
  188.0 62.5 %copy-start.3 = (bf16[32]{0:T(256)(128)(2,1)}, bf16[32]{0:T(256)(128)(2,1)S(1)}, u32[]{:S(2)}) copy-start(bf16[32]{0:T(256)(128)(2,1)S(1)} %fusion.143) | copy-start | bytes 196
  250.4 0.8 copy-start
  722.3 1.5 copy-start.1
  722.3 1.5 copy-start.4
  723.8 7.3 copy-start.5
  725.1 16.0 %all-to-all-start.2 = ((bf16[16,2,4096]{2,1,0:T(2,128)(2,1)}), bf16[16,2,4096]{2,1,0:T(2,128)(2,1)S(1)}, u32[]{:S(2)}, u32[]{:S(2)}) async-start(bf16[16,2,4096]{2,1,0:T(2,128)(2,1)} %reshape.126), calls=%async_computation.2 | async-start | bytes 524288 | tf_op jit(solution)/shard_map/all_to_all | solution.py:124
  731.2 10.9 %copy-start.6 = (s32[32]{0:T(128)S(1)}, s32[32]{0:T(128)}, u32[]{:S(2)}) copy-start(s32[32]{0:T(128)} %get-tuple-element.627) | copy-start | bytes 388
where the time goes:
time: 760 us; the launch traced here: 753 us
  matrix products  397 us (52%)
  local copies, waits for them, and re-layouts  259 us (34%)
  other arithmetic  54.1 us (7%)
  starting transfers between devices  19.4 us (3%)
  loops' own time  13.6 us (2%)
  waiting for transfers between devices  9.96 us (1%)
    dot_general x257, matrix products, mix(): return jnp.einsum(form, first, second, preferred_element_type=jnp.float32)  391 us
    gather x288, local copies, waits for them, and re-layouts  228 us
    convert_element_type x16, other arithmetic, one_wave(): field_im = (amplitude * sine).astype(jnp.bfloat16)  46.9 us
    dynamic_slice x16, local copies, waits for them, and re-layouts, one_wave(): wavelength = wavelengths[wave_idx]  20.2 us
  transfers between devices with their start and end apart: 3, of which 1 were waited for; matrix products, arithmetic and copies ran while one was open for 31% of the time, Pallas kernels for 0%

commit v1 on v0

v1 whole, which is shorter than its diff:
```python
import functools
import math

import jax
import jax.numpy as jnp
from jax import lax
from jax.experimental import pallas as pl
from jax.experimental.pallas import tpu as pltpu
from jax.sharding import PartitionSpec as P

SUB = 64
LANES = 2 * SUB
HEAD = 16
WINDOW = SUB + 8
FIELDS = 5
SAMPLING = 0.5
GROUP = 2
UNROLL = 4
VMEM_LIMIT = 48 * 1024 * 1024

SINE = (4.442882919124343, -7.308245686509023, 3.6063542184319086, -0.8461116503677503, 0.10982451641387822)
COSINE = (1.4142134962552284, -6.978850948563799, 5.7394603769067665, -1.8835579059841794, 0.3106880275221932)


def horner(coefficients, z):
    total = coefficients[-1]
    for coefficient in coefficients[-2::-1]:
        total = total * z + coefficient
    return total


def half_turn(turns):
    r = turns - jnp.round(turns)
    z = r * r
    return horner(SINE, z) * r, horner(COSINE, z)


def row_limit(rows, first, extent):
    i = lax.broadcasted_iota(jnp.int32, (rows, LANES), 0) + first
    down = jnp.abs(2 * i - (extent - 1))
    return jnp.where(8 * down <= 7 * (extent - 1), 7 * (extent - 1) - 4 * down, -1)


def aligned(row, extent):
    base = pl.multiple_of(jnp.minimum(row // 8 * 8, extent - WINDOW), 8)
    return base, row - base


def sideways(first, extent):
    j = lax.broadcasted_iota(jnp.int32, (1, LANES), 1) + first
    return 7 * jnp.abs(2 * j - (extent - 1))


def cut_kernel(table, maps, out, masked):
    peers = out.shape[0]
    segs, extent, _ = maps.shape
    chunk = 32
    for row in range(0, extent, chunk):
        limit = row_limit(chunk, row, extent)
        for half in range(extent // LANES):
            inside = sideways(half * LANES, extent) <= limit
            for s in range(segs):
                spot = (s, pl.ds(row, chunk), pl.ds(half * LANES, LANES))
                masked[spot] = jnp.where(inside, maps[spot].astype(jnp.float32), 0.0)
    lane = lax.broadcasted_iota(jnp.int32, (SUB, LANES), 1)
    tall_lane = lax.broadcasted_iota(jnp.int32, (WINDOW, LANES), 1)
    head_lane = lax.broadcasted_iota(jnp.int32, (HEAD, LANES), 1)

    def one_peer(p, carry):
        head = jnp.zeros((HEAD, LANES), jnp.int32)
        sides = []
        for c in range(2):
            live, seg, row, col = (table[p, c, k] for k in (0, 1, 3, 4))
            base, down = aligned(row, extent)
            left = masked[seg, pl.ds(base, WINDOW), pl.ds(0, LANES)]
            right = masked[seg, pl.ds(base, WINDOW), pl.ds(LANES, LANES)]
            both = jnp.where(tall_lane >= col, left, right)
            both = pltpu.roll(both, jnp.where(down == 0, 0, WINDOW - down), axis=0)[:SUB]
            both = pltpu.roll(both, (2 * LANES + SUB * c - col) & (LANES - 1), axis=1)
            sides.append(both * live.astype(jnp.float32))
            for k in range(FIELDS):
                head = jnp.where(head_lane == FIELDS * c + k, table[p, c, k], head)
        out[p, pl.ds(0, SUB), :] = jnp.where(lane < SUB, sides[0], sides[1]).astype(jnp.bfloat16)
        out[p, pl.ds(SUB, HEAD), :] = head.astype(jnp.float32).astype(jnp.bfloat16)
        return carry

    lax.fori_loop(0, peers, one_peer, 0, unroll=2)


def wave_kernel(
    extent, waves_ref, message, cotangent, out,
    heads, table, place, slot_place, owner_of, opd, amplitude, grad, turns_per, left1, left2, right1, right2, sem,
):
    peers = message.shape[0]
    waves = waves_ref.shape[0]
    lenses, focal, _ = cotangent.shape
    pairs = opd.shape[0] - 1
    dead_place = 2 * pairs

    def one_head(p, carry):
        heads[pl.ds(p, 1), :] = message[p, pl.ds(SUB, HEAD), :].astype(jnp.float32)[0:1].astype(jnp.int32)
        return carry

    lax.fori_loop(0, peers, one_head, 0, unroll=4)
    copy = pltpu.make_async_copy(heads, table, sem)
    copy.start()

    opd[...] = jnp.zeros_like(opd)
    amplitude[...] = jnp.zeros_like(amplitude)

    position = lax.broadcasted_iota(jnp.int32, (focal, LANES), 0) - focal // 2
    lane = lax.broadcasted_iota(jnp.int32, (SUB, LANES), 1)
    across = lane % SUB - SUB // 2
    product = (position * across).astype(jnp.float32)
    lower = lane < SUB

    def one_table(w, carry):
        inverse = 1.0 / jnp.full((8, LANES), waves_ref[w], jnp.float32)
        turns_per[w] = inverse
        sine, cosine = half_turn(product * (-SAMPLING / SUB) * inverse[0:1])
        real = 1.0 - sine * sine
        imag = sine * cosine
        zero = jnp.zeros_like(real)
        left1[w, pl.ds(0, SUB), :] = jnp.where(lower, real, -imag).astype(jnp.bfloat16)
        left1[w, pl.ds(SUB, SUB), :] = jnp.where(lower, imag, real).astype(jnp.bfloat16)
        left2[w, pl.ds(0, SUB), :] = jnp.where(lower, real, imag).astype(jnp.bfloat16)
        left2[w, pl.ds(SUB, SUB), :] = jnp.where(lower, -imag, real).astype(jnp.bfloat16)
        for h in range(2):
            own = lower if h == 0 else ~lower
            re = jnp.where(own, real, zero).astype(jnp.bfloat16)
            im = jnp.where(own, imag, zero)
            minus = (-im).astype(jnp.bfloat16)
            im = im.astype(jnp.bfloat16)
            first = pl.ds(h * SUB, SUB)
            second = pl.ds(LANES + h * SUB, SUB)
            right1[w, first, pl.ds(0, LANES)] = re
            right1[w, first, pl.ds(LANES, LANES)] = im
            right1[w, second, pl.ds(0, LANES)] = minus
            right1[w, second, pl.ds(LANES, LANES)] = re
            right2[w, first, pl.ds(0, LANES)] = re
            right2[w, first, pl.ds(LANES, LANES)] = minus
            right2[w, second, pl.ds(0, LANES)] = im
            right2[w, second, pl.ds(LANES, LANES)] = re
        return carry

    lax.fori_loop(0, waves, one_table, 0)

    def clear(l, carry):
        place[l] = -1
        owner_of[l] = 0
        return carry

    lax.fori_loop(0, lenses, clear, 0)
    copy.wait()

    def one_slot(p, count):
        patch = message[p, pl.ds(0, SUB), :].astype(jnp.float32)
        for c in range(2):
            live = table[p, FIELDS * c] == 1
            lens, row, col = (table[p, FIELDS * c + k] for k in (2, 3, 4))
            before = place[lens]
            fresh = live & (before < 0)
            here = jnp.where(fresh, count, before)
            place[lens] = here
            owner_of[count] = jnp.where(fresh, lens, 0)
            count = count + fresh.astype(jnp.int32)
            here = jnp.where(live, here, dead_place)
            slot_place[2 * p + c] = here
            pair = here // 2
            half = here % 2
            own = lane // SUB == half
            moved = pltpu.roll(patch, SUB * jnp.where(half == c, 0, 1), axis=1)
            opd[pair] += jnp.where(own, moved, 0.0)
            inside = own & (sideways(col - SUB * half, extent) <= row_limit(SUB, row, extent))
            amplitude[pair] += jnp.where(inside, 1.0, 0.0)
        return count

    count = lax.fori_loop(0, peers, one_slot, 0)

    def one_group(g, carry):
        weights = []
        for i in range(GROUP):
            k = g * (2 * GROUP) + 2 * i
            pieces = [cotangent[owner_of[k + h]].astype(jnp.float32) for h in range(2)]
            weights.append(jnp.concatenate(pieces, axis=1) * (2.0 / (waves * SUB)))
            grad[g * GROUP + i] = jnp.zeros((SUB, LANES), jnp.float32)

        def one_wave(w):
            scale = turns_per[w][0:1]
            reals, imags = [], []
            for i in range(GROUP):
                amp = amplitude[g * GROUP + i]
                sine, cosine = half_turn(opd[g * GROUP + i] * scale)
                part = amp * sine
                reals.append(amp - part * sine)
                imags.append(part * cosine)

            def stack(res, ims):
                top = jnp.concatenate([x.astype(jnp.bfloat16) for x in res], axis=1)
                low = jnp.concatenate([x.astype(jnp.bfloat16) for x in ims], axis=1)
                return jnp.concatenate([top, low], axis=0)

            def line(x):
                x = x.astype(jnp.bfloat16)
                rows = []
                for i in range(GROUP):
                    at = slice(LANES * i, LANES * (i + 1))
                    rows.append(jnp.concatenate([x[:SUB, at], x[SUB:, at]], axis=1))
                return jnp.concatenate(rows, axis=0)

            p = jnp.dot(left1[w], stack(reals, imags), preferred_element_type=jnp.float32)
            f = jnp.dot(line(p), right1[w], preferred_element_type=jnp.float32)
            held = [[], []]
            for i in range(GROUP):
                for h in range(2):
                    held[h].append(f[SUB * i : SUB * (i + 1), LANES * h : LANES * (h + 1)] * weights[i])
            q = jnp.dot(left2[w], stack(*held), preferred_element_type=jnp.float32)
            b = jnp.dot(line(q), right2[w], preferred_element_type=jnp.float32)
            factor = scale * (2.0 * math.pi / SUB)
            for i in range(GROUP):
                back = b[SUB * i : SUB * (i + 1)]
                grad[g * GROUP + i] += factor * (reals[i] * back[:, LANES:] - imags[i] * back[:, :LANES])

        def some_waves(step, inner):
            for u in range(UNROLL):
                one_wave(step * UNROLL + u)
            return inner

        lax.fori_loop(0, waves // UNROLL, some_waves, 0)
        return carry

    lax.fori_loop(0, (count + 2 * GROUP - 1) // (2 * GROUP), one_group, 0)

    def one_return(p, carry):
        sides = []
        for c in range(2):
            here = slot_place[2 * p + c]
            row, col = table[p, FIELDS * c + 3], table[p, FIELDS * c + 4]
            pair = here // 2
            half = here % 2
            moved = pltpu.roll(grad[pair], SUB * jnp.where(half == c, 0, 1), axis=1)
            reach = jnp.where(here < dead_place, row_limit(SUB, row, extent), -1)
            sides.append(jnp.where(sideways(col - SUB * c, extent) <= reach, moved, 0.0))
        out[p] = jnp.where(lower, sides[0], sides[1]).astype(jnp.bfloat16)
        return carry

    lax.fori_loop(0, peers, one_return, 0, unroll=2)


def place_kernel(table, patches, out):
    peers = patches.shape[0]
    extent = out.shape[1]
    lane = lax.broadcasted_iota(jnp.int32, (WINDOW, LANES), 1)
    spare = jnp.zeros((WINDOW - SUB, LANES), jnp.float32)
    out[...] = jnp.zeros_like(out)

    def one_peer(p, carry):
        both = jnp.concatenate([patches[p].astype(jnp.float32), spare], axis=0)
        for c in range(2):
            seg, row, col = (table[p, c, k] for k in (1, 3, 4))
            base, down = aligned(row, extent)
            moved = pltpu.roll(both, (col + LANES - SUB * c) & (LANES - 1), axis=1)
            moved = pltpu.roll(moved, down, axis=0)
            for half in range(2):
                j = lane + (half * LANES - col)
                kept = jnp.where((j >= 0) & (j < SUB), moved, 0.0)
                spot = (seg, pl.ds(base, WINDOW), pl.ds(half * LANES, LANES))
                out[spot] += kept
        return carry

    lax.fori_loop(0, peers, one_peer, 0)


def on_device(segment_maps, cotangent, wavelengths, intersections):
    peers = intersections.shape[0]
    waves = wavelengths.shape[0]
    lenses = cotangent.shape[0]
    segs, extent, _ = segment_maps.shape
    pairs = -(-lenses // (2 * GROUP)) * GROUP
    vmem = pl.BlockSpec(memory_space=pltpu.VMEM)
    smem = pl.BlockSpec(memory_space=pltpu.SMEM)
    params = pltpu.CompilerParams(vmem_limit_bytes=VMEM_LIMIT)

    message = pl.pallas_call(
        cut_kernel,
        out_shape=jax.ShapeDtypeStruct((peers, SUB + HEAD, LANES), jnp.bfloat16),
        in_specs=[smem, vmem],
        out_specs=vmem,
        scratch_shapes=[pltpu.VMEM((segs, extent, extent), jnp.float32)],
        compiler_params=params,
        name="cut_patches",
    )(intersections, segment_maps)
    arriving = lax.all_to_all(message, "tile", split_axis=0, concat_axis=0, tiled=True)
    grads = pl.pallas_call(
        functools.partial(wave_kernel, extent),
        out_shape=jax.ShapeDtypeStruct((peers, SUB, LANES), jnp.bfloat16),
        in_specs=[smem, vmem, vmem],
        out_specs=vmem,
        scratch_shapes=[
            pltpu.VMEM((peers, LANES), jnp.int32),
            pltpu.SMEM((peers, LANES), jnp.int32),
            pltpu.SMEM((lenses,), jnp.int32),
            pltpu.SMEM((2 * peers,), jnp.int32),
            pltpu.SMEM((2 * pairs + 1,), jnp.int32),
            pltpu.VMEM((pairs + 1, SUB, LANES), jnp.float32),
            pltpu.VMEM((pairs + 1, SUB, LANES), jnp.float32),
            pltpu.VMEM((pairs + 1, SUB, LANES), jnp.float32),
            pltpu.VMEM((waves, 8, LANES), jnp.float32),
            pltpu.VMEM((waves, LANES, LANES), jnp.bfloat16),
            pltpu.VMEM((waves, LANES, LANES), jnp.bfloat16),
            pltpu.VMEM((waves, 2 * LANES, 2 * LANES), jnp.bfloat16),
            pltpu.VMEM((waves, 2 * LANES, 2 * LANES), jnp.bfloat16),
            pltpu.SemaphoreType.DMA,
        ],
        compiler_params=params,
        name="wave_gradients",
    )(wavelengths, arriving, cotangent)
    returned = lax.all_to_all(grads, "tile", split_axis=0, concat_axis=0, tiled=True)
    return pl.pallas_call(
        place_kernel,
        out_shape=jax.ShapeDtypeStruct((segs, extent, extent), jnp.float32),
        in_specs=[smem, vmem],
        out_specs=vmem,
        compiler_params=params,
        name="place_gradients",
    )(intersections, returned)


def solution(mesh):
    return jax.shard_map(
        on_device,
        mesh=mesh,
        in_specs=(
            P(("case", "tile"), None, None),
            P(("case", "tile"), None, None),
            P(),
            P(("case", "tile"), None, None),
        ),
        out_specs=P(("case", "tile"), None, None),
        check_vma=False,
    )
```

time: 760 us -> 75.4 us (0.10)
  matrix products: 397 us -> 0 us
  local copies, waits for them, and re-layouts: 259 us -> 1.83 us
  other arithmetic: 54.1 us -> 0 us
  Pallas kernels: 0 us -> 36.7 us
  blocking collectives: 0 us -> 36.7 us
  starting transfers between devices: 19.4 us -> 0 us
  loops' own time: 13.6 us -> 0 us
  waiting for transfers between devices: 9.96 us -> 0 us
    dot_general x264 -> x0, matrix products: 397 us -> none  [the longest x257 391 us: mix(): return jnp.einsum(form, first, second, preferred_element_type=jnp.float32)]
    gather x290 -> x0, local copies, waits for them, and re-layouts: 229 us -> none
    convert_element_type x18 -> x0, other arithmetic: 47.1 us -> none  [the longest x16 46.9 us: one_wave(): field_im = (amplitude * sine).astype(jnp.bfloat16)]
    pallas_call x0 -> x3, Pallas kernels: none -> 36.7 us  [the longest x1 31.2 us: on_device(): pl.pallas_call(functools.partial(wave_kernel, extent), out_shape=jax.Shap...]
    all_to_all x0 -> x2, blocking collectives: none -> 36.7 us  [the longest x1 18.4 us: on_device(): lax.all_to_all(message, 'tile', split_axis=0, concat_axis=0, tiled=True)]
    dynamic_slice x20 -> x0, local copies, waits for them, and re-layouts: 22.6 us -> none  [the longest x16 20.2 us: one_wave(): wavelength = wavelengths[wave_idx]]
    all_to_all x3 -> x0, starting transfers between devices: 19.4 us -> none  [the longest x1 7.39 us: on_device(): lax.all_to_all(intersections, 'tile', split_axis=0, concat_axis=0, tiled=...]
    another operation x5 -> x0, loops' own time: 13.6 us -> none  [the longest x1 12.2 us: on_device(): lax.fori_loop(0, waves, one_wave, jnp.zeros((lens_count, pupil, pupil), j...]
  transfers between devices with their start and end apart: 3 -> 0, of which waited for: 1 -> 0; matrix products, arithmetic and copies ran while one was open for 31% -> 0% of each run, Pallas kernels for 0% -> 0%
where the time goes in v1:
time: 75.4 us; the launch traced here: 75.3 us
  Pallas kernels  36.7 us (49%)
  blocking collectives  36.7 us (49%)
  local copies, waits for them, and re-layouts  1.83 us (2%)
    pallas_call x1, Pallas kernels, on_device(): pl.pallas_call(functools.partial(wave_kernel, extent), out_shape=jax.Shap...  31.2 us
    all_to_all x1, blocking collectives, on_device(): lax.all_to_all(message, 'tile', split_axis=0, concat_axis=0, tiled=True)  18.4 us
    all_to_all x1, blocking collectives, on_device(): lax.all_to_all(grads, 'tile', split_axis=0, concat_axis=0, tiled=True)  18.3 us
    pallas_call x1, Pallas kernels, on_device(): pl.pallas_call(place_kernel, out_shape=jax.ShapeDtypeStruct((segs, extent...  3.48 us
    pallas_call x1, Pallas kernels, on_device(): pl.pallas_call(cut_kernel, out_shape=jax.ShapeDtypeStruct((peers, SUB + H...  2.02 us
    unnamed x7, local copies, waits for them, and re-layouts  1.83 us

profile of v1, /device:TPU:0, one launch (start us, length us, event | category | flops | bytes accessed | tf_op | source)
XLA Modules:
  0.0 75.3 jit_solution(3036264394125881239)
XLA Ops:
  0.0 0.8 %copy.6.table = s32[16,2,5]{2,1,0:T(2,128)S(1)} copy(s32[16,2,5]{0,1,2:T(2,128)} %param.7) | data formatting | bytes 1280 | tf_op args[3]
  0.8 0.0 copy-start
  0.8 1.0 %copy-done = bf16[4,256,256]{2,1,0:T(8,128)(2,1)S(1)} copy-done((bf16[4,256,256]{2,1,0:T(8,128)(2,1)S(1)}, bf16[4,256,256]{2,1,0:T(8,128)(2,1)}, u32[]{:S(2)}) %copy-start) | copy-done | bytes 524312
  1.8 2.0 %cut_patches.1 = bf16[16,80,128]{2,1,0:T(8,128)(2,1)S(1)} custom-call(s32[16,2,5]{2,1,0:T(2,128)S(1)} %copy.6.table, bf16[4,256,256]{2,1,0:T(8,128)(2,1)S(1)} %copy-done), custom_call_target="tpu_custom_call" | custom-call | tf_op jit(solution)/shard_map/cut_patches/pallas_call | solution.py:284
  3.8 0.0 copy-start.1
  3.9 0.0 copy-start.2
  3.9 18.4 %all_to_all.10.message = bf16[16,80,128]{2,1,0:T(8,128)(2,1)S(1)} all-to-all(bf16[16,80,128]{2,1,0:T(8,128)(2,1)S(1)} %cut_patches.1), channel_id=1, replica_groups=mesh['case'=2,'tile'=16] {'tile'}, dimensions={0} | all-to-all | bytes 655360 | tf_op jit(solution)/shard_map/all_to_all | solution.py:293
  22.3 0.0 copy-done.1
  22.3 0.0 copy-done.2
  22.3 31.2 %wave_gradients.1 = bf16[16,64,128]{2,1,0:T(8,128)(2,1)S(1)} custom-call(f32[16]{0:T(128)S(1)} %copy-done.2, bf16[16,80,128]{2,1,0:T(8,128)(2,1)S(1)} %all_to_all.10.message, bf16[24,64,64]{2,1,0:T(8,128)(2,1)S(1)} %copy-done.1), custom_call_target="tpu_custom_call" | custom-call | tf_op jit(solution)/shard_map/wave_gradients/pallas_call | solution.py:294
  53.5 18.3 %all_to_all.11.patches = bf16[16,64,128]{2,1,0:T(8,128)(2,1)S(1)} all-to-all(bf16[16,64,128]{2,1,0:T(8,128)(2,1)S(1)} %wave_gradients.1), channel_id=1, replica_groups=mesh['case'=2,'tile'=16] {'tile'}, dimensions={0} | all-to-all | bytes 524288 | tf_op jit(solution)/shard_map/all_to_all | solution.py:318
  71.8 3.5 %place_gradients.1 = f32[4,256,256]{2,1,0:T(8,128)} custom-call(s32[16,2,5]{2,1,0:T(2,128)S(1)} %copy.6.table, bf16[16,64,128]{2,1,0:T(8,128)(2,1)S(1)} %all_to_all.11.patches), custom_call_target="tpu_custom_call" | custom-call | tf_op jit(solution)/shard_map/place_gradients/pallas_call | solution.py:319
Async XLA Ops:
  0.8 1.0 %copy-start = (bf16[4,256,256]{2,1,0:T(8,128)(2,1)S(1)}, bf16[4,256,256]{2,1,0:T(8,128)(2,1)}, u32[]{:S(2)}) copy-start(bf16[4,256,256]{2,1,0:T(8,128)(2,1)} %maps.1) | copy-start | bytes 1572868
  3.8 18.4 %copy-start.1 = (bf16[24,64,64]{2,1,0:T(8,128)(2,1)S(1)}, bf16[24,64,64]{2,1,0:T(8,128)(2,1)}, u32[]{:S(2)}) copy-start(bf16[24,64,64]{2,1,0:T(8,128)(2,1)} %cotangent.1) | copy-start | bytes 589828
  3.9 18.4 %copy-start.2 = (f32[16]{0:T(128)S(1)}, f32[16]{0:T(128)}, u32[]{:S(2)}) copy-start(f32[16]{0:T(128)} %waves_ref.1) | copy-start | bytes 196

commit v2 on v1

--- a/solution.py
+++ b/solution.py
@@ -10,12 +10,13 @@
 
 SUB = 64
 LANES = 2 * SUB
-HEAD = 16
+HEAD = 8
 WINDOW = SUB + 8
 FIELDS = 5
 SAMPLING = 0.5
-GROUP = 2
-UNROLL = 4
+GROUP = 4
+UNROLL = 16
+ORDER = (0, 1, 2, 3, 4)
 VMEM_LIMIT = 48 * 1024 * 1024
 
 SINE = (4.442882919124343, -7.308245686509023, 3.6063542184319086, -0.8461116503677503, 0.10982451641387822)
@@ -185,7 +186,20 @@
             weights.append(jnp.concatenate(pieces, axis=1) * (2.0 / (waves * SUB)))
             grad[g * GROUP + i] = jnp.zeros((SUB, LANES), jnp.float32)
 
-        def one_wave(w):
+        def stack(res, ims):
+            top = jnp.concatenate([x.astype(jnp.bfloat16) for x in res], axis=1)
+            low = jnp.concatenate([x.astype(jnp.bfloat16) for x in ims], axis=1)
+            return jnp.concatenate([top, low], axis=0)
+
+        def line(x):
+            x = x.astype(jnp.bfloat16)
+            rows = []
+            for i in range(GROUP):
+                at = slice(LANES * i, LANES * (i + 1))
+                rows.append(jnp.concatenate([x[:SUB, at], x[SUB:, at]], axis=1))
+            return jnp.concatenate(rows, axis=0)
+
+        def field(w):
             scale = turns_per[w][0:1]
             reals, imags = [], []
             for i in range(GROUP):
@@ -194,36 +208,42 @@
                 part = amp * sine
                 reals.append(amp - part * sine)
                 imags.append(part * cosine)
-
-            def stack(res, ims):
-                top = jnp.concatenate([x.astype(jnp.bfloat16) for x in res], axis=1)
-                low = jnp.concatenate([x.astype(jnp.bfloat16) for x in ims], axis=1)
-                return jnp.concatenate([top, low], axis=0)
-
-            def line(x):
-                x = x.astype(jnp.bfloat16)
-                rows = []
-                for i in range(GROUP):
-                    at = slice(LANES * i, LANES * (i + 1))
-                    rows.append(jnp.concatenate([x[:SUB, at], x[SUB:, at]], axis=1))
-                return jnp.concatenate(rows, axis=0)
-
-            p = jnp.dot(left1[w], stack(reals, imags), preferred_element_type=jnp.float32)
-            f = jnp.dot(line(p), right1[w], preferred_element_type=jnp.float32)
+            return reals, imags, stack(reals, imags)
+
+        def pupil_rows(w, state):
+            reals, imags, e = state
+            return reals, imags, line(jnp.dot(left1[w], e, preferred_element_type=jnp.float32))
+
+        def pupil_columns(w, state):
+            reals, imags, p = state
+            f = jnp.dot(p, right1[w], preferred_element_type=jnp.float32)
             held = [[], []]
             for i in range(GROUP):
                 for h in range(2):
                     held[h].append(f[SUB * i : SUB * (i + 1), LANES * h : LANES * (h + 1)] * weights[i])
-            q = jnp.dot(left2[w], stack(*held), preferred_element_type=jnp.float32)
-            b = jnp.dot(line(q), right2[w], preferred_element_type=jnp.float32)
-            factor = scale * (2.0 * math.pi / SUB)
+            return reals, imags, stack(*held)
+
+        def focal_rows(w, state):
+            reals, imags, held = state
+            return reals, imags, line(jnp.dot(left2[w], held, preferred_element_type=jnp.float32))
+
+        def focal_columns(w, state):
+            reals, imags, q = state
+            b = jnp.dot(q, right2[w], preferred_element_type=jnp.float32)
+            factor = turns_per[w][0:1] * (2.0 * math.pi / SUB)
             for i in range(GROUP):
                 back = b[SUB * i : SUB * (i + 1)]
                 grad[g * GROUP + i] += factor * (reals[i] * back[:, LANES:] - imags[i] * back[:, :LANES])
 
         def some_waves(step, inner):
-            for u in range(UNROLL):
-                one_wave(step * UNROLL + u)
+            stages = (pupil_rows, pupil_columns, focal_rows, focal_columns)
+            states = {}
+            for t in range(UNROLL + len(stages)):
+                for k in ORDER:
+                    u = t - k
+                    if 0 <= u < UNROLL:
+                        w = step * UNROLL + u
+                        states[u] = field(w) if k == 0 else stages[k - 1](w, states[u])
             return inner
 
         lax.fori_loop(0, waves // UNROLL, some_waves, 0)
@@ -247,51 +267,14 @@
     lax.fori_loop(0, peers, one_return, 0, unroll=2)
 
 
-def place_kernel(table, patches, out):
-    peers = patches.shape[0]
-    extent = out.shape[1]
-    lane = lax.broadcasted_iota(jnp.int32, (WINDOW, LANES), 1)
-    spare = jnp.zeros((WINDOW - SUB, LANES), jnp.float32)
-    out[...] = jnp.zeros_like(out)
-
-    def one_peer(p, carry):
-        both = jnp.concatenate([patches[p].astype(jnp.float32), spare], axis=0)
-        for c in range(2):
-            seg, row, col = (table[p, c, k] for k in (1, 3, 4))
-            base, down = aligned(row, extent)
-            moved = pltpu.roll(both, (col + LANES - SUB * c) & (LANES - 1), axis=1)
-            moved = pltpu.roll(moved, down, axis=0)
-            for half in range(2):
-                j = lane + (half * LANES - col)
-                kept = jnp.where((j >= 0) & (j < SUB), moved, 0.0)
-                spot = (seg, pl.ds(base, WINDOW), pl.ds(half * LANES, LANES))
-                out[spot] += kept
-        return carry
-
-    lax.fori_loop(0, peers, one_peer, 0)
-
-
-def on_device(segment_maps, cotangent, wavelengths, intersections):
-    peers = intersections.shape[0]
+def wave_call(wavelengths, message, cotangent, extent):
+    peers = message.shape[0]
     waves = wavelengths.shape[0]
     lenses = cotangent.shape[0]
-    segs, extent, _ = segment_maps.shape
     pairs = -(-lenses // (2 * GROUP)) * GROUP
     vmem = pl.BlockSpec(memory_space=pltpu.VMEM)
     smem = pl.BlockSpec(memory_space=pltpu.SMEM)
-    params = pltpu.CompilerParams(vmem_limit_bytes=VMEM_LIMIT)
-
-    message = pl.pallas_call(
-        cut_kernel,
-        out_shape=jax.ShapeDtypeStruct((peers, SUB + HEAD, LANES), jnp.bfloat16),
-        in_specs=[smem, vmem],
-        out_specs=vmem,
-        scratch_shapes=[pltpu.VMEM((segs, extent, extent), jnp.float32)],
-        compiler_params=params,
-        name="cut_patches",
-    )(intersections, segment_maps)
-    arriving = lax.all_to_all(message, "tile", split_axis=0, concat_axis=0, tiled=True)
-    grads = pl.pallas_call(
+    return pl.pallas_call(
         functools.partial(wave_kernel, extent),
         out_shape=jax.ShapeDtypeStruct((peers, SUB, LANES), jnp.bfloat16),
         in_specs=[smem, vmem, vmem],
@@ -312,9 +295,53 @@
             pltpu.VMEM((waves, 2 * LANES, 2 * LANES), jnp.bfloat16),
             pltpu.SemaphoreType.DMA,
         ],
+        compiler_params=pltpu.CompilerParams(vmem_limit_bytes=VMEM_LIMIT),
+        name="wave_gradients",
+    )(wavelengths, message, cotangent)
+
+
+def place_kernel(table, patches, out):
+    peers = patches.shape[0]
+    extent = out.shape[1]
+    lane = lax.broadcasted_iota(jnp.int32, (WINDOW, LANES), 1)
+    spare = jnp.zeros((WINDOW - SUB, LANES), jnp.float32)
+    out[...] = jnp.zeros_like(out)
+
+    def one_peer(p, carry):
+        both = jnp.concatenate([patches[p].astype(jnp.float32), spare], axis=0)
+        for c in range(2):
+            seg, row, col = (table[p, c, k] for k in (1, 3, 4))
+            base, down = aligned(row, extent)
+            moved = pltpu.roll(both, (col + LANES - SUB * c) & (LANES - 1), axis=1)
+            moved = pltpu.roll(moved, down, axis=0)
+            for half in range(2):
+                j = lane + (half * LANES - col)
+                kept = jnp.where((j >= 0) & (j < SUB), moved, 0.0)
+                spot = (seg, pl.ds(base, WINDOW), pl.ds(half * LANES, LANES))
+                out[spot] += kept
+        return carry
+
+    lax.fori_loop(0, peers, one_peer, 0)
+
+
+def on_device(segment_maps, cotangent, wavelengths, intersections):
+    peers = intersections.shape[0]
+    segs, extent, _ = segment_maps.shape
+    vmem = pl.BlockSpec(memory_space=pltpu.VMEM)
+    smem = pl.BlockSpec(memory_space=pltpu.SMEM)
+    params = pltpu.CompilerParams(vmem_limit_bytes=VMEM_LIMIT)
+
+    message = pl.pallas_call(
+        cut_kernel,
+        out_shape=jax.ShapeDtypeStruct((peers, SUB + HEAD, LANES), jnp.bfloat16),
+        in_specs=[smem, vmem],
+        out_specs=vmem,
+        scratch_shapes=[pltpu.VMEM((segs, extent, extent), jnp.float32)],
         compiler_params=params,
-        name="wave_gradients",
-    )(wavelengths, arriving, cotangent)
+        name="cut_patches",
+    )(intersections, segment_maps)
+    arriving = lax.all_to_all(message, "tile", split_axis=0, concat_axis=0, tiled=True)
+    grads = wave_call(wavelengths, arriving, cotangent, extent)
     returned = lax.all_to_all(grads, "tile", split_axis=0, concat_axis=0, tiled=True)
     return pl.pallas_call(
         place_kernel,

time: 75.4 us -> 53 us (0.70); the launches traced: 75.3 us -> 52.1 us
  Pallas kernels: 36.7 us -> 17.3 us
  blocking collectives: 36.7 us -> 32.9 us
    pallas_call x1, Pallas kernels: 31.2 us -> 11.8 us  [wave_call(): pl.pallas_call(functools.partial(wave_kernel, extent), out_shape=jax.Shap...]
    all_to_all x1, blocking collectives: 18.3 us -> 15 us  [on_device(): lax.all_to_all(grads, 'tile', split_axis=0, concat_axis=0, tiled=True)]
where the time goes in v2:
time: 53 us; the launch traced here: 52.1 us
  blocking collectives  32.9 us (62%)
  Pallas kernels  17.3 us (33%)
  local copies, waits for them, and re-layouts  1.83 us (3%)
    all_to_all x1, blocking collectives, on_device(): lax.all_to_all(message, 'tile', split_axis=0, concat_axis=0, tiled=True)  17.9 us
    all_to_all x1, blocking collectives, on_device(): lax.all_to_all(grads, 'tile', split_axis=0, concat_axis=0, tiled=True)  15 us
    pallas_call x1, Pallas kernels, wave_call(): pl.pallas_call(functools.partial(wave_kernel, extent), out_shape=jax.Shap...  11.8 us
    pallas_call x1, Pallas kernels, on_device(): pl.pallas_call(place_kernel, out_shape=jax.ShapeDtypeStruct((segs, extent...  3.48 us
    pallas_call x1, Pallas kernels, on_device(): pl.pallas_call(cut_kernel, out_shape=jax.ShapeDtypeStruct((peers, SUB + H...  2.01 us
    unnamed x7, local copies, waits for them, and re-layouts  1.83 us

profile of v2, /device:TPU:0, one launch (start us, length us, event | category | flops | bytes accessed | tf_op | source)
XLA Modules:
  0.0 52.1 jit_solution(9018559201234452389)
XLA Ops:
  0.0 0.8 %copy.6.table = s32[16,2,5]{2,1,0:T(2,128)S(1)} copy(s32[16,2,5]{0,1,2:T(2,128)} %param.7) | data formatting | bytes 1280 | tf_op args[3]
  0.8 0.0 copy-start
  0.8 1.0 %copy-done = bf16[4,256,256]{2,1,0:T(8,128)(2,1)S(1)} copy-done((bf16[4,256,256]{2,1,0:T(8,128)(2,1)S(1)}, bf16[4,256,256]{2,1,0:T(8,128)(2,1)}, u32[]{:S(2)}) %copy-start) | copy-done | bytes 524312
  1.8 2.0 %cut_patches.1 = bf16[16,72,128]{2,1,0:T(8,128)(2,1)S(1)} custom-call(s32[16,2,5]{2,1,0:T(2,128)S(1)} %copy.6.table, bf16[4,256,256]{2,1,0:T(8,128)(2,1)S(1)} %copy-done), custom_call_target="tpu_custom_call" | custom-call | tf_op jit(solution)/shard_map/cut_patches/pallas_call | solution.py:334
  3.8 0.0 copy-start.1
  3.8 0.0 copy-start.2
  3.9 17.9 %all_to_all.10.message = bf16[16,72,128]{2,1,0:T(8,128)(2,1)S(1)} all-to-all(bf16[16,72,128]{2,1,0:T(8,128)(2,1)S(1)} %cut_patches.1), channel_id=1, replica_groups=mesh['case'=2,'tile'=16] {'tile'}, dimensions={0} | all-to-all | bytes 589824 | tf_op jit(solution)/shard_map/all_to_all | solution.py:343
  21.7 0.0 copy-done.1
  21.8 0.0 copy-done.2
  21.8 11.8 %wave_gradients.1 = bf16[16,64,128]{2,1,0:T(8,128)(2,1)S(1)} custom-call(f32[16]{0:T(128)S(1)} %copy-done.2, bf16[16,72,128]{2,1,0:T(8,128)(2,1)S(1)} %all_to_all.10.message, bf16[24,64,64]{2,1,0:T(8,128)(2,1)S(1)} %copy-done.1), custom_call_target="tpu_custom_call" | custom-call | tf_op jit(solution)/shard_map/wave_gradients/pallas_call | solution.py:277
  33.6 15.0 %all_to_all.11.patches = bf16[16,64,128]{2,1,0:T(8,128)(2,1)S(1)} all-to-all(bf16[16,64,128]{2,1,0:T(8,128)(2,1)S(1)} %wave_gradients.1), channel_id=1, replica_groups=mesh['case'=2,'tile'=16] {'tile'}, dimensions={0} | all-to-all | bytes 524288 | tf_op jit(solution)/shard_map/all_to_all | solution.py:345
  48.6 3.5 %place_gradients.1 = f32[4,256,256]{2,1,0:T(8,128)} custom-call(s32[16,2,5]{2,1,0:T(2,128)S(1)} %copy.6.table, bf16[16,64,128]{2,1,0:T(8,128)(2,1)S(1)} %all_to_all.11.patches), custom_call_target="tpu_custom_call" | custom-call | tf_op jit(solution)/shard_map/place_gradients/pallas_call | solution.py:346
Async XLA Ops:
  0.8 1.0 %copy-start = (bf16[4,256,256]{2,1,0:T(8,128)(2,1)S(1)}, bf16[4,256,256]{2,1,0:T(8,128)(2,1)}, u32[]{:S(2)}) copy-start(bf16[4,256,256]{2,1,0:T(8,128)(2,1)} %maps.1) | copy-start | bytes 1572868
  3.8 17.9 %copy-start.1 = (bf16[24,64,64]{2,1,0:T(8,128)(2,1)S(1)}, bf16[24,64,64]{2,1,0:T(8,128)(2,1)}, u32[]{:S(2)}) copy-start(bf16[24,64,64]{2,1,0:T(8,128)(2,1)} %cotangent.1) | copy-start | bytes 589828
  3.8 17.9 %copy-start.2 = (f32[16]{0:T(128)S(1)}, f32[16]{0:T(128)}, u32[]{:S(2)}) copy-start(f32[16]{0:T(128)} %waves_ref.1) | copy-start | bytes 196

commit v3 on v2

v3 whole, which is shorter than its diff:
```python
import functools
import math

import jax
import jax.numpy as jnp
from jax import lax
from jax.experimental import pallas as pl
from jax.experimental.pallas import tpu as pltpu
from jax.sharding import PartitionSpec as P

SUB = 64
LANES = 2 * SUB
HEAD = 8
WINDOW = SUB + 8
FIELDS = 5
SAMPLING = 0.5
GROUP = 4
GROUP_FEW = 5
FEW = 20
VMEM_LIMIT = 48 * 1024 * 1024

LEAD = -0.7843722149521581
SINE = tuple(a / LEAD for a in (4.442867901299065, -7.307443351304121, 3.594787401596918))
COSINE = tuple(a / LEAD for a in (1.4142040792740376, -6.9776419299271595, 5.715236658714806, -1.7283430271755356))


FINE_SINE = (4.442882834139933, -7.308241153900929, 3.6062889473067714, -0.8457635292158341, 0.10920561913977103)
FINE_COSINE = (1.4142134965588182, -6.978850987079529, 5.739461141869117, -1.8835627683436942, 0.3106976855933321)


def horner(coefficients, z):
    total = coefficients[-1]
    for coefficient in coefficients[-2::-1]:
        total = total * z + coefficient
    return total


def half_turn(turns):
    r = turns - jnp.round(turns)
    z = r * r
    sine = (((z + SINE[2]) * z + SINE[1]) * z + SINE[0]) * r
    cosine = ((COSINE[3] * z + COSINE[2]) * z + COSINE[1]) * z + COSINE[0]
    return sine, cosine


def row_limit(rows, first, extent):
    i = lax.broadcasted_iota(jnp.int32, (rows, LANES), 0) + first
    down = jnp.abs(2 * i - (extent - 1))
    return jnp.where(8 * down <= 7 * (extent - 1), 7 * (extent - 1) - 4 * down, -1)


def aligned(row, extent):
    base = pl.multiple_of(jnp.minimum(row // 8 * 8, extent - WINDOW), 8)
    return base, row - base


def sideways(first, extent):
    j = lax.broadcasted_iota(jnp.int32, (1, LANES), 1) + first
    return 7 * jnp.abs(2 * j - (extent - 1))


def window(image, row, col, extent, side):
    base, down = aligned(row, extent)
    left = image[pl.ds(base, WINDOW), pl.ds(0, LANES)]
    right = image[pl.ds(base, WINDOW), pl.ds(LANES, LANES)]
    lane = lax.broadcasted_iota(jnp.int32, (WINDOW, LANES), 1)
    both = jnp.where(lane >= col, left, right)
    both = pltpu.roll(both, jnp.where(down == 0, 0, WINDOW - down), axis=0)[:SUB]
    return pltpu.roll(both, (2 * LANES + SUB * side - col) & (LANES - 1), axis=1)


def fill_mask(mask):
    extent = mask.shape[0]
    chunk = 32
    for row in range(0, extent, chunk):
        limit = row_limit(chunk, row, extent)
        for half in range(extent // LANES):
            inside = sideways(half * LANES, extent) <= limit
            mask[pl.ds(row, chunk), pl.ds(half * LANES, LANES)] = jnp.where(inside, 1.0, 0.0)


def read_table(entries, heads, table, sem):
    for p in range(entries.shape[0]):
        heads[pl.ds(2 * p, 2), pl.ds(0, FIELDS)] = entries[p]
    copy = pltpu.make_async_copy(heads, table, sem)
    copy.start()
    return copy


def cut_kernel(entries, maps, out, heads, table, raw, masked, sem, map_sems):
    peers = out.shape[0]
    segs, extent, _ = maps.shape
    loads = [pltpu.make_async_copy(maps.at[s], raw.at[s], map_sems.at[s]) for s in range(segs)]
    for load in loads:
        load.start()
    copy = read_table(entries, heads, table, sem)
    lower = lax.broadcasted_iota(jnp.int32, (SUB, LANES), 1) < SUB
    for p in range(peers):
        out[p, pl.ds(SUB, HEAD), :] = jnp.zeros((HEAD, LANES), jnp.bfloat16)
        out[p, pl.ds(SUB, 2), pl.ds(0, FIELDS)] = entries[p].astype(jnp.float32).astype(jnp.bfloat16)
    chunk = 32
    for s in range(segs):
        loads[s].wait()
        for row in range(0, extent, chunk):
            limit = row_limit(chunk, row, extent)
            for half in range(extent // LANES):
                inside = sideways(half * LANES, extent) <= limit
                spot = (s, pl.ds(row, chunk), pl.ds(half * LANES, LANES))
                masked[spot] = jnp.where(inside, raw[spot].astype(jnp.float32), 0.0)
    copy.wait()

    def one_peer(p, carry):
        sides = []
        for c in range(2):
            live, seg, row, col = (table[2 * p + c, k] for k in (0, 1, 3, 4))
            piece = window(masked.at[seg], row, col, extent, c)
            sides.append(piece * live.astype(jnp.float32))
        out[p, pl.ds(0, SUB), :] = jnp.where(lower, sides[0], sides[1]).astype(jnp.bfloat16)
        return carry

    lax.fori_loop(0, peers, one_peer, 0, unroll=8)


def table_kernel(waves_ref, turns_per, left1, left2, right1, right2):
    waves = waves_ref.shape[0]
    position = lax.broadcasted_iota(jnp.int32, (SUB, LANES), 0) - SUB // 2
    lane = lax.broadcasted_iota(jnp.int32, (SUB, LANES), 1)
    across = (lane & (SUB - 1)) - SUB // 2
    product = (position * across).astype(jnp.float32) * (-SAMPLING / SUB)
    lower = lane < SUB

    def one_table(w, carry):
        inverse = 1.0 / jnp.full((8, LANES), waves_ref[w], jnp.float32)
        turns_per[w] = inverse
        turns = product * inverse[0:1]
        r = turns - jnp.round(turns)
        z = r * r
        sine = horner(FINE_SINE, z) * r
        real = 1.0 - sine * sine
        imag = sine * horner(FINE_COSINE, z)
        zero = jnp.zeros_like(real)
        left1[w, pl.ds(0, SUB), :] = jnp.where(lower, real, -imag).astype(jnp.bfloat16)
        left1[w, pl.ds(SUB, SUB), :] = jnp.where(lower, imag, real).astype(jnp.bfloat16)
        left2[w, pl.ds(0, SUB), :] = jnp.where(lower, real, imag).astype(jnp.bfloat16)
        left2[w, pl.ds(SUB, SUB), :] = jnp.where(lower, -imag, real).astype(jnp.bfloat16)
        for h in range(2):
            own = lower if h == 0 else ~lower
            re = jnp.where(own, real, zero).astype(jnp.bfloat16)
            im = jnp.where(own, imag, zero)
            minus = (-im).astype(jnp.bfloat16)
            im = im.astype(jnp.bfloat16)
            first = pl.ds(h * SUB, SUB)
            second = pl.ds(LANES + h * SUB, SUB)
            right1[w, first, pl.ds(0, LANES)] = re
            right1[w, first, pl.ds(LANES, LANES)] = im
            right1[w, second, pl.ds(0, LANES)] = minus
            right1[w, second, pl.ds(LANES, LANES)] = re
            right2[w, first, pl.ds(0, LANES)] = re
            right2[w, first, pl.ds(LANES, LANES)] = minus
            right2[w, second, pl.ds(0, LANES)] = im
            right2[w, second, pl.ds(LANES, LANES)] = re
        return carry

    lax.fori_loop(0, waves, one_table, 0)


def table_call(wavelengths):
    waves = wavelengths.shape[0]
    vmem = pl.BlockSpec(memory_space=pltpu.VMEM)
    return pl.pallas_call(
        table_kernel,
        out_shape=[
            jax.ShapeDtypeStruct((waves, 8, LANES), jnp.float32),
            jax.ShapeDtypeStruct((waves, LANES, LANES), jnp.bfloat16),
            jax.ShapeDtypeStruct((waves, LANES, LANES), jnp.bfloat16),
            jax.ShapeDtypeStruct((waves, 2 * LANES, 2 * LANES), jnp.bfloat16),
            jax.ShapeDtypeStruct((waves, 2 * LANES, 2 * LANES), jnp.bfloat16),
        ],
        in_specs=[pl.BlockSpec(memory_space=pltpu.SMEM)],
        out_specs=[vmem] * 5,
        compiler_params=pltpu.CompilerParams(vmem_limit_bytes=VMEM_LIMIT),
        cost_estimate=pl.CostEstimate(flops=10_000_000, bytes_accessed=6_000_000, transcendentals=0),
        name="lens_tables",
    )(wavelengths)


def wave_groups(group, count, owner_of, cotangent, opd, amplitude, grad, turns_per, left1, left2, right1, right2):
    waves = turns_per.shape[0]

    def stack(res, ims):
        top = jnp.concatenate([x.astype(jnp.bfloat16) for x in res], axis=1)
        low = jnp.concatenate([x.astype(jnp.bfloat16) for x in ims], axis=1)
        return jnp.concatenate([top, low], axis=0)

    def line(x):
        x = x.astype(jnp.bfloat16)
        rows = []
        for i in range(group):
            at = slice(LANES * i, LANES * (i + 1))
            rows.append(jnp.concatenate([x[:SUB, at], x[SUB:, at]], axis=1))
        return jnp.concatenate(rows, axis=0)

    def one_group(g, carry):
        weights, scaled = [], []
        totals = [None] * group
        for i in range(group):
            k = (g * group + i) * 2
            pieces = [cotangent[owner_of[k + h]].astype(jnp.float32) for h in range(2)]
            scaled.append(amplitude[g * group + i] * LEAD**2)
            weights.append(jnp.concatenate(pieces, axis=1) * (2.0 / (waves * SUB)))

        def field(w, state):
            scale = turns_per[w][0:1]
            reals, imags = [], []
            for i in range(group):
                sine, cosine = half_turn(opd[g * group + i] * scale)
                part = scaled[i] * sine
                reals.append(amplitude[g * group + i] - part * sine)
                imags.append(part * cosine)
            return reals, imags, stack(reals, imags)

        def pupil_rows(w, state):
            reals, imags, e = state
            return reals, imags, line(jnp.dot(left1[w], e, preferred_element_type=jnp.float32))

        def pupil_columns(w, state):
            reals, imags, p = state
            f = jnp.dot(p, right1[w], preferred_element_type=jnp.float32)
            held = [[], []]
            for i in range(group):
                for h in range(2):
                    held[h].append(f[SUB * i : SUB * (i + 1), LANES * h : LANES * (h + 1)] * weights[i])
            return reals, imags, stack(*held)

        def focal_rows(w, state):
            reals, imags, held = state
            return reals, imags, line(jnp.dot(left2[w], held, preferred_element_type=jnp.float32))

        def focal_columns(w, state):
            reals, imags, q = state
            b = jnp.dot(q, right2[w], preferred_element_type=jnp.float32)
            factor = turns_per[w][0:1] * (2.0 * math.pi / SUB)
            for i in range(group):
                back = b[SUB * i : SUB * (i + 1)]
                term = factor * (reals[i] * back[:, LANES:] - imags[i] * back[:, :LANES])
                totals[i] = term if totals[i] is None else totals[i] + term

        stages = (field, pupil_rows, pupil_columns, focal_rows, focal_columns)
        states = [None] * waves
        for t in range(waves + len(stages) - 1):
            for k, stage in enumerate(stages):
                if 0 <= t - k < waves:
                    states[t - k] = stage(t - k, states[t - k])
        for i in range(group):
            grad[g * group + i] = totals[i]
        return carry

    lax.fori_loop(0, (count + 2 * group - 1) // (2 * group), one_group, 0)


def wave_kernel(
    message, cotangent, turns_far, left1_far, left2_far, right1_far, right2_far, out,
    turns_per, left1, left2, right1, right2,
    heads, table, place, slot_place, owner_of, opd, amplitude, grad, shades, mask, sem, table_sems,
):
    peers = message.shape[0]
    lenses = cotangent.shape[0]
    pairs = opd.shape[0] - 1
    extent = mask.shape[0]
    dead_place = 2 * pairs

    far = (turns_far, left1_far, right1_far, left2_far, right2_far)
    near = (turns_per, left1, right1, left2, right2)
    loads = [pltpu.make_async_copy(x, y, table_sems.at[i]) for i, (x, y) in enumerate(zip(far, near))]
    for load in loads:
        load.start()
    for p in range(peers):
        head = message[p, pl.ds(SUB, HEAD), :].astype(jnp.float32)[0:2]
        heads[pl.ds(2 * p, 2), :] = head.astype(jnp.int32)
    copy = pltpu.make_async_copy(heads, table, sem)
    copy.start()
    fill_mask(mask)
    opd[...] = jnp.zeros_like(opd)
    amplitude[...] = jnp.zeros_like(amplitude)
    lane = lax.broadcasted_iota(jnp.int32, (SUB, LANES), 1)
    lower = lane < SUB
    for l in range(lenses):
        place[l] = -1
    for k in range(dead_place + 1):
        owner_of[k] = 0
    copy.wait()

    def one_place(i, count):
        live = table[i, 0] == 1
        lens = table[i, 2]
        before = place[lens]
        fresh = live & (before < 0)
        here = jnp.where(fresh, count, before)
        place[lens] = here
        owner_of[count] = jnp.where(fresh, lens, 0)
        slot_place[i] = jnp.where(live, here, dead_place)
        return count + fresh.astype(jnp.int32)

    count = lax.fori_loop(0, 2 * peers, one_place, 0, unroll=4)

    def one_slot(p, carry):
        patch = message[p, pl.ds(0, SUB), :].astype(jnp.float32)
        sides = []
        for c in range(2):
            live, row, col = (table[2 * p + c, k] for k in (0, 3, 4))
            sides.append(window(mask, row, col, extent, c) * live.astype(jnp.float32))
        shade = jnp.where(lower, sides[0], sides[1])
        shades[p] = shade
        for c in range(2):
            here = slot_place[2 * p + c]
            pair = here >> 1
            half = here & 1
            turn = (half ^ c) * SUB
            own = (lane >> 6) == half
            opd[pair] += jnp.where(own, pltpu.roll(patch, turn, axis=1), 0.0)
            amplitude[pair] += jnp.where(own, pltpu.roll(shade, turn, axis=1), 0.0)
        return carry

    lax.fori_loop(0, peers, one_slot, 0, unroll=4)
    for load in loads:
        load.wait()

    arrays = (owner_of, cotangent, opd, amplitude, grad, turns_per, left1, left2, right1, right2)
    few = count <= FEW

    @pl.when(few)
    def _():
        wave_groups(GROUP_FEW, count, *arrays)

    @pl.when(jnp.logical_not(few))
    def _():
        wave_groups(GROUP, count, *arrays)

    def one_return(p, carry):
        sides = []
        for c in range(2):
            here = slot_place[2 * p + c]
            sides.append(pltpu.roll(grad[here >> 1], ((here & 1) ^ c) * SUB, axis=1))
        picked = jnp.where(lower, sides[0], sides[1])
        out[p] = jnp.where(shades[p] > 0.0, picked, 0.0).astype(jnp.bfloat16)
        return carry

    lax.fori_loop(0, peers, one_return, 0, unroll=4)


def round_up(value, step):
    return -(-value // step) * step


def wave_call(tables, message, cotangent, extent):
    peers = message.shape[0]
    lenses = cotangent.shape[0]
    pairs = max(round_up(lenses, 2 * GROUP), round_up(lenses, 2 * GROUP_FEW)) // 2
    vmem = pl.BlockSpec(memory_space=pltpu.VMEM)
    far = pl.BlockSpec(memory_space=pltpu.HBM)
    return pl.pallas_call(
        wave_kernel,
        out_shape=jax.ShapeDtypeStruct((peers, SUB, LANES), jnp.bfloat16),
        in_specs=[vmem, vmem] + [far] * len(tables),
        out_specs=vmem,
        scratch_shapes=[pltpu.VMEM(x.shape, x.dtype) for x in tables] + [
            pltpu.VMEM((2 * peers, LANES), jnp.int32),
            pltpu.SMEM((2 * peers, LANES), jnp.int32),
            pltpu.SMEM((lenses,), jnp.int32),
            pltpu.SMEM((2 * peers,), jnp.int32),
            pltpu.SMEM((2 * pairs + 1,), jnp.int32),
            pltpu.VMEM((pairs + 1, SUB, LANES), jnp.float32),
            pltpu.VMEM((pairs + 1, SUB, LANES), jnp.float32),
            pltpu.VMEM((pairs + 1, SUB, LANES), jnp.float32),
            pltpu.VMEM((peers, SUB, LANES), jnp.float32),
            pltpu.VMEM((extent, extent), jnp.float32),
            pltpu.SemaphoreType.DMA,
            pltpu.SemaphoreType.DMA((len(tables),)),
        ],
        compiler_params=pltpu.CompilerParams(vmem_limit_bytes=VMEM_LIMIT),
        name="wave_gradients",
    )(message, cotangent, *tables)


def place_kernel(entries, patches, out, heads, table, sem):
    peers = patches.shape[0]
    extent = out.shape[1]
    copy = read_table(entries, heads, table, sem)
    lane = lax.broadcasted_iota(jnp.int32, (WINDOW, LANES), 1)
    spare = jnp.zeros((WINDOW - SUB, LANES), jnp.float32)
    out[...] = jnp.zeros_like(out)
    copy.wait()

    def one_peer(p, carry):
        both = jnp.concatenate([patches[p].astype(jnp.float32), spare], axis=0)
        for c in range(2):
            seg, row, col = (table[2 * p + c, k] for k in (1, 3, 4))
            base, down = aligned(row, extent)
            moved = pltpu.roll(both, (col + LANES - SUB * c) & (LANES - 1), axis=1)
            moved = pltpu.roll(moved, down, axis=0)
            for half in range(2):
                j = lane + (half * LANES - col)
                kept = jnp.where((j >= 0) & (j < SUB), moved, 0.0)
                spot = (seg, pl.ds(base, WINDOW), pl.ds(half * LANES, LANES))
                out[spot] += kept
        return carry

    lax.fori_loop(0, peers, one_peer, 0, unroll=4)


def on_device(segment_maps, cotangent, wavelengths, intersections):
    peers = intersections.shape[0]
    segs, extent, _ = segment_maps.shape
    vmem = pl.BlockSpec(memory_space=pltpu.VMEM)
    table_space = [pltpu.VMEM((2 * peers, LANES), jnp.int32), pltpu.SMEM((2 * peers, LANES), jnp.int32)]
    params = pltpu.CompilerParams(vmem_limit_bytes=VMEM_LIMIT)

    message = pl.pallas_call(
        cut_kernel,
        out_shape=jax.ShapeDtypeStruct((peers, SUB + HEAD, LANES), jnp.bfloat16),
        in_specs=[vmem, pl.BlockSpec(memory_space=pltpu.HBM)],
        out_specs=vmem,
        scratch_shapes=[
            *table_space,
            pltpu.VMEM((segs, extent, extent), jnp.bfloat16),
            pltpu.VMEM((segs, extent, extent), jnp.float32),
            pltpu.SemaphoreType.DMA,
            pltpu.SemaphoreType.DMA((segs,)),
        ],
        compiler_params=params,
        name="cut_patches",
    )(intersections, segment_maps)
    tables = table_call(wavelengths)
    arriving = lax.all_to_all(message, "tile", split_axis=0, concat_axis=0, tiled=True)
    grads = wave_call(tables, arriving, cotangent, extent)
    returned = lax.all_to_all(grads, "tile", split_axis=0, concat_axis=0, tiled=True)
    return pl.pallas_call(
        place_kernel,
        out_shape=jax.ShapeDtypeStruct((segs, extent, extent), jnp.float32),
        in_specs=[vmem, vmem],
        out_specs=vmem,
        scratch_shapes=[*table_space, pltpu.SemaphoreType.DMA],
        compiler_params=params,
        name="place_gradients",
    )(intersections, returned)


def solution(mesh):
    return jax.shard_map(
        on_device,
        mesh=mesh,
        in_specs=(
            P(("case", "tile"), None, None),
            P(("case", "tile"), None, None),
            P(),
            P(("case", "tile"), None, None),
        ),
        out_specs=P(("case", "tile"), None, None),
        check_vma=False,
    )
```

time: 53 us -> 50.2 us (0.947); the launches traced: 52.1 us -> 50 us
  blocking collectives: 32.9 us -> 16.9 us
  starting transfers between devices: 0 us -> 7.4 us
  waiting for transfers between devices: 0 us -> 6.79 us
  Pallas kernels: 17.3 us -> 14 us
  local copies, waits for them, and re-layouts: 1.83 us -> 4.81 us
    all_to_all x1 -> x0, blocking collectives: 17.9 us -> none  [on_device(): lax.all_to_all(message, 'tile', split_axis=0, concat_axis=0, tiled=True)]
    all_to_all x0 -> x1, starting transfers between devices: none -> 7.4 us  [on_device(): lax.all_to_all(message, 'tile', split_axis=0, concat_axis=0, tiled=True)]
    all_to_all x0 -> x1, waiting for transfers between devices: none -> 6.79 us  [on_device(): lax.all_to_all(message, 'tile', split_axis=0, concat_axis=0, tiled=True)]
    pallas_call x1 -> x2, Pallas kernels: 11.8 us -> 8.63 us  [the longest x1 6.86 us: wave_call(): pl.pallas_call(wave_kernel, out_shape=jax.ShapeDtypeStruct((peers, SUB, L...]
    unnamed x7 -> x9, local copies, waits for them, and re-layouts: 1.83 us -> 4.81 us
    all_to_all x1, blocking collectives: 15 us -> 16.9 us  [on_device(): lax.all_to_all(grads, 'tile', split_axis=0, concat_axis=0, tiled=True)]
    pallas_call x1, Pallas kernels: 3.48 us -> 2.59 us  [on_device(): pl.pallas_call(place_kernel, out_shape=jax.ShapeDtypeStruct((segs, extent...]
    pallas_call x1, Pallas kernels: 2.01 us -> 2.79 us  [on_device(): pl.pallas_call(cut_kernel, out_shape=jax.ShapeDtypeStruct((peers, SUB + H...]
  transfers between devices with their start and end apart: 0 -> 1, of which waited for: 0 -> 1; matrix products, arithmetic and copies ran while one was open for 0% -> 0% of each run, Pallas kernels for 0% -> 4%
where the time goes in v3:
time: 50.2 us; the launch traced here: 50 us
  blocking collectives  16.9 us (34%)
  Pallas kernels  14 us (28%)
  starting transfers between devices  7.4 us (15%)
  waiting for transfers between devices  6.79 us (14%)
  local copies, waits for them, and re-layouts  4.81 us (10%)
    all_to_all x1, blocking collectives, on_device(): lax.all_to_all(grads, 'tile', split_axis=0, concat_axis=0, tiled=True)  16.9 us
    all_to_all x1, starting transfers between devices, on_device(): lax.all_to_all(message, 'tile', split_axis=0, concat_axis=0, tiled=True)  7.4 us
    pallas_call x1, Pallas kernels, wave_call(): pl.pallas_call(wave_kernel, out_shape=jax.ShapeDtypeStruct((peers, SUB, L...  6.86 us
    all_to_all x1, waiting for transfers between devices, on_device(): lax.all_to_all(message, 'tile', split_axis=0, concat_axis=0, tiled=True)  6.79 us
    unnamed x9, local copies, waits for them, and re-layouts  4.81 us
    pallas_call x1, Pallas kernels, on_device(): pl.pallas_call(cut_kernel, out_shape=jax.ShapeDtypeStruct((peers, SUB + H...  2.79 us
    pallas_call x1, Pallas kernels, on_device(): pl.pallas_call(place_kernel, out_shape=jax.ShapeDtypeStruct((segs, extent...  2.59 us
    pallas_call x1, Pallas kernels, table_call(): pl.pallas_call(table_kernel, out_shape=[jax.ShapeDtypeStruct((waves, 8, L...  1.77 us
  transfers between devices with their start and end apart: 1, of which 1 were waited for; matrix products, arithmetic and copies ran while one was open for 0% of the time, Pallas kernels for 4%

profile of v3, /device:TPU:0, one launch (start us, length us, event | category | flops | bytes accessed | tf_op | source)
XLA Modules:
  0.0 50.0 jit_solution(10160881103710635411)
XLA Ops:
  0.0 0.8 %copy.6.entries = s32[16,2,5]{2,1,0:T(2,128)S(1)} copy(s32[16,2,5]{0,1,2:T(2,128)} %param.7) | data formatting | bytes 1280 | tf_op args[3]
  0.8 0.0 copy-start.1
  0.8 1.0 %copy-done.1 = bf16[4,256,256]{2,1,0:T(8,128)(2,1)S(1)} copy-done((bf16[4,256,256]{2,1,0:T(8,128)(2,1)S(1)}, bf16[4,256,256]{2,1,0:T(8,128)(2,1)}, u32[]{:S(2)}) %copy-start.1) | copy-done | bytes 524312
  1.8 2.8 %cut_patches.1 = bf16[16,72,128]{2,1,0:T(8,128)(2,1)} custom-call(s32[16,2,5]{2,1,0:T(2,128)S(1)} %copy.6.entries, bf16[4,256,256]{2,1,0:T(8,128)(2,1)S(1)} %copy-done.1), custom_call_target="tpu_custom_call" | custom-call | tf_op jit(solution)/shard_map/cut_patches/pallas_call | solution.py:418
  4.6 7.4 %all-to-all-start = ((bf16[16,72,128]{2,1,0:T(8,128)(2,1)}), bf16[16,72,128]{2,1,0:T(8,128)(2,1)S(1)}, u32[]{:S(2)}, u32[]{:S(2)}) async-start(bf16[16,72,128]{2,1,0:T(8,128)(2,1)} %cut_patches.1), calls=%async_computation | async-start | bytes 589824 | tf_op jit(solution)/shard_map/all_to_all | solution.py:434
  12.0 0.0 copy-start.3
  12.0 0.6 %copy-done.3 = f32[16]{0:T(128)S(1)} copy-done((f32[16]{0:T(128)S(1)}, f32[16]{0:T(128)}, u32[]{:S(2)}) %copy-start.3) | copy-done | bytes 88
  12.7 1.8 %lens_tables.1 = (f32[16,8,128]{2,1,0:T(8,128)S(1)}, bf16[16,128,128]{2,1,0:T(8,128)(2,1)S(1)}, bf16[16,128,128]{2,1,0:T(8,128)(2,1)S(1)}, bf16[16,256,256]{2,1,0:T(8,128)(2,1)S(1)}, bf16[16,256,256]{2,1,0:T(8,128)(2,1)S(1)}) custom-call(f32[16]{0:T(128)S(1)} %copy-done.3), custom_call_target="tpu_custom_call" | custom-call | flops 10000000 | bytes 6000000 | tf_op jit(solution)/shard_map/lens_tables/pallas_call | solution.py:170
  14.5 0.0 copy-start
  14.5 1.3 %copy-done = bf16[16,256,256]{2,1,0:T(8,128)(2,1)} copy-done((bf16[16,256,256]{2,1,0:T(8,128)(2,1)}, bf16[16,256,256]{2,1,0:T(8,128)(2,1)S(1)}, u32[]{:S(2)}) %copy-start) | copy-done | bytes 2097176
  15.8 6.8 %all-to-all-done.message = bf16[16,72,128]{2,1,0:T(8,128)(2,1)S(1)} async-done(((bf16[16,72,128]{2,1,0:T(8,128)(2,1)}), bf16[16,72,128]{2,1,0:T(8,128)(2,1)S(1)}, u32[]{:S(2)}, u32[]{:S(2)}) %all-to-all-start) | async-done | bytes 294944 | tf_op jit(solution)/shard_map/all_to_all | solution.py:434
  22.6 0.0 copy-start.2
  22.6 1.0 %copy-done.2 = bf16[24,64,64]{2,1,0:T(8,128)(2,1)S(1)} copy-done((bf16[24,64,64]{2,1,0:T(8,128)(2,1)S(1)}, bf16[24,64,64]{2,1,0:T(8,128)(2,1)}, u32[]{:S(2)}) %copy-start.2) | copy-done | bytes 196632
  23.6 6.9 %wave_gradients.1 = bf16[16,64,128]{2,1,0:T(8,128)(2,1)S(1)} custom-call(bf16[16,72,128]{2,1,0:T(8,128)(2,1)S(1)} %all-to-all-done.message, bf16[24,64,64]{2,1,0:T(8,128)(2,1)S(1)} %copy-done.2, f32[16,8,128]{2,1,0:T(8,128)S(1)} %get-tuple-element.10.turns_far, bf16[16,128,128]{2,1,0:T(8,128)(2,1)S(1)} %get-tuple-element.11.left1_far, ...), custom_call_target="tpu_custom_call" | custom-call | tf_op jit(solution)/shard_map/wave_gradients/pallas_call | solution.py:361
  30.5 16.9 %all_to_all.10.patches = bf16[16,64,128]{2,1,0:T(8,128)(2,1)S(1)} all-to-all(bf16[16,64,128]{2,1,0:T(8,128)(2,1)S(1)} %wave_gradients.1), channel_id=1, replica_groups=mesh['case'=2,'tile'=16] {'tile'}, dimensions={0} | all-to-all | bytes 524288 | tf_op jit(solution)/shard_map/all_to_all | solution.py:436
  47.4 2.6 %place_gradients.1 = f32[4,256,256]{2,1,0:T(8,128)} custom-call(s32[16,2,5]{2,1,0:T(2,128)S(1)} %copy.6.entries, bf16[16,64,128]{2,1,0:T(8,128)(2,1)S(1)} %all_to_all.10.patches), custom_call_target="tpu_custom_call" | custom-call | tf_op jit(solution)/shard_map/place_gradients/pallas_call | solution.py:437
Async XLA Ops:
  0.8 1.0 %copy-start.1 = (bf16[4,256,256]{2,1,0:T(8,128)(2,1)S(1)}, bf16[4,256,256]{2,1,0:T(8,128)(2,1)}, u32[]{:S(2)}) copy-start(bf16[4,256,256]{2,1,0:T(8,128)(2,1)} %maps.1) | copy-start | bytes 1572868
  4.6 18.0 %all-to-all-start = ((bf16[16,72,128]{2,1,0:T(8,128)(2,1)}), bf16[16,72,128]{2,1,0:T(8,128)(2,1)S(1)}, u32[]{:S(2)}, u32[]{:S(2)}) async-start(bf16[16,72,128]{2,1,0:T(8,128)(2,1)} %cut_patches.1), calls=%async_computation | async-start | bytes 589824 | tf_op jit(solution)/shard_map/all_to_all | solution.py:434
  12.0 0.7 %copy-start.3 = (f32[16]{0:T(128)S(1)}, f32[16]{0:T(128)}, u32[]{:S(2)}) copy-start(f32[16]{0:T(128)} %waves_ref.1) | copy-start | bytes 196
  14.5 1.4 %copy-start = (bf16[16,256,256]{2,1,0:T(8,128)(2,1)}, bf16[16,256,256]{2,1,0:T(8,128)(2,1)S(1)}, u32[]{:S(2)}) copy-start(bf16[16,256,256]{2,1,0:T(8,128)(2,1)S(1)} %get-tuple-element.14.right2_far) | copy-start | bytes 6291460
  22.6 1.0 %copy-start.2 = (bf16[24,64,64]{2,1,0:T(8,128)(2,1)S(1)}, bf16[24,64,64]{2,1,0:T(8,128)(2,1)}, u32[]{:S(2)}) copy-start(bf16[24,64,64]{2,1,0:T(8,128)(2,1)} %cotangent.1) | copy-start | bytes 589828

commit v4 on v3

--- a/solution.py
+++ b/solution.py
@@ -11,13 +11,17 @@
 SUB = 64
 LANES = 2 * SUB
 HEAD = 8
+HEAD_ROWS = 16
 WINDOW = SUB + 8
+RIGHT1, RIGHT2, LEFT, WAVE_ROWS = 0, 2 * LANES, 4 * LANES, 5 * LANES
 FIELDS = 5
 SAMPLING = 0.5
 GROUP = 4
 GROUP_FEW = 5
 FEW = 20
+VMEM = 64 * 1024 * 1024
 VMEM_LIMIT = 48 * 1024 * 1024
+FAR_ROWS = 40960
 
 LEAD = -0.7843722149521581
 SINE = tuple(a / LEAD for a in (4.442867901299065, -7.307443351304121, 3.594787401596918))
@@ -80,24 +84,27 @@
 
 
 def read_table(entries, heads, table, sem):
-    for p in range(entries.shape[0]):
-        heads[pl.ds(2 * p, 2), pl.ds(0, FIELDS)] = entries[p]
+    for k in range(FIELDS):
+        heads[pl.ds(2 * k, 2), pl.ds(0, entries.shape[2])] = entries[k]
     copy = pltpu.make_async_copy(heads, table, sem)
     copy.start()
     return copy
 
 
-def cut_kernel(entries, maps, out, heads, table, raw, masked, sem, map_sems):
+def cut_kernel(entries_far, maps, out, entries, heads, table, raw, masked, sem, map_sems):
     peers = out.shape[0]
     segs, extent, _ = maps.shape
+    first = pltpu.make_async_copy(entries_far, entries, sem)
+    first.start()
     loads = [pltpu.make_async_copy(maps.at[s], raw.at[s], map_sems.at[s]) for s in range(segs)]
     for load in loads:
         load.start()
+    lower = lax.broadcasted_iota(jnp.int32, (SUB, LANES), 1) < SUB
+    first.wait()
     copy = read_table(entries, heads, table, sem)
-    lower = lax.broadcasted_iota(jnp.int32, (SUB, LANES), 1) < SUB
+    rows = jnp.transpose(heads[...].astype(jnp.float32)).astype(jnp.bfloat16)
     for p in range(peers):
-        out[p, pl.ds(SUB, HEAD), :] = jnp.zeros((HEAD, LANES), jnp.bfloat16)
-        out[p, pl.ds(SUB, 2), pl.ds(0, FIELDS)] = entries[p].astype(jnp.float32).astype(jnp.bfloat16)
+        out[p, pl.ds(SUB, 1), pl.ds(0, HEAD_ROWS)] = rows[p : p + 1]
     chunk = 32
     for s in range(segs):
         loads[s].wait()
@@ -112,7 +119,7 @@
     def one_peer(p, carry):
         sides = []
         for c in range(2):
-            live, seg, row, col = (table[2 * p + c, k] for k in (0, 1, 3, 4))
+            live, seg, row, col = (table[2 * k + c, p] for k in (0, 1, 3, 4))
             piece = window(masked.at[seg], row, col, extent, c)
             sides.append(piece * live.astype(jnp.float32))
         out[p, pl.ds(0, SUB), :] = jnp.where(lower, sides[0], sides[1]).astype(jnp.bfloat16)
@@ -121,7 +128,15 @@
     lax.fori_loop(0, peers, one_peer, 0, unroll=8)
 
 
-def table_kernel(waves_ref, turns_per, left1, left2, right1, right2):
+def slab_rows(waves, lenses):
+    return waves * WAVE_ROWS + round_up(lenses, 2) // 2 * SUB
+
+
+def weight_spot(lens, waves):
+    return pl.ds(waves * WAVE_ROWS + (lens >> 1) * SUB, SUB), pl.ds(pl.multiple_of((lens & 1) * LANES, LANES), LANES)
+
+
+def table_kernel(waves_ref, cotangent, slab_far, slab, sem):
     waves = waves_ref.shape[0]
     position = lax.broadcasted_iota(jnp.int32, (SUB, LANES), 0) - SUB // 2
     lane = lax.broadcasted_iota(jnp.int32, (SUB, LANES), 1)
@@ -130,62 +145,62 @@
     lower = lane < SUB
 
     def one_table(w, carry):
-        inverse = 1.0 / jnp.full((8, LANES), waves_ref[w], jnp.float32)
-        turns_per[w] = inverse
-        turns = product * inverse[0:1]
+        turns = product * (1.0 / jnp.full((1, LANES), waves_ref[w], jnp.float32))
         r = turns - jnp.round(turns)
         z = r * r
         sine = horner(FINE_SINE, z) * r
         real = 1.0 - sine * sine
         imag = sine * horner(FINE_COSINE, z)
-        zero = jnp.zeros_like(real)
-        left1[w, pl.ds(0, SUB), :] = jnp.where(lower, real, -imag).astype(jnp.bfloat16)
-        left1[w, pl.ds(SUB, SUB), :] = jnp.where(lower, imag, real).astype(jnp.bfloat16)
-        left2[w, pl.ds(0, SUB), :] = jnp.where(lower, real, imag).astype(jnp.bfloat16)
-        left2[w, pl.ds(SUB, SUB), :] = jnp.where(lower, -imag, real).astype(jnp.bfloat16)
+
+        def put(row, side, value):
+            slab[pl.ds(w * WAVE_ROWS + row, SUB), pl.ds(side * LANES, LANES)] = value.astype(jnp.bfloat16)
+
+        put(LEFT, 0, jnp.where(lower, real, -imag))
+        put(LEFT + SUB, 0, jnp.where(lower, imag, real))
+        put(LEFT, 1, jnp.where(lower, real, imag))
+        put(LEFT + SUB, 1, jnp.where(lower, -imag, real))
         for h in range(2):
             own = lower if h == 0 else ~lower
-            re = jnp.where(own, real, zero).astype(jnp.bfloat16)
-            im = jnp.where(own, imag, zero)
-            minus = (-im).astype(jnp.bfloat16)
-            im = im.astype(jnp.bfloat16)
-            first = pl.ds(h * SUB, SUB)
-            second = pl.ds(LANES + h * SUB, SUB)
-            right1[w, first, pl.ds(0, LANES)] = re
-            right1[w, first, pl.ds(LANES, LANES)] = im
-            right1[w, second, pl.ds(0, LANES)] = minus
-            right1[w, second, pl.ds(LANES, LANES)] = re
-            right2[w, first, pl.ds(0, LANES)] = re
-            right2[w, first, pl.ds(LANES, LANES)] = minus
-            right2[w, second, pl.ds(0, LANES)] = im
-            right2[w, second, pl.ds(LANES, LANES)] = re
+            re = jnp.where(own, real, 0.0)
+            im = jnp.where(own, imag, 0.0)
+            first, second = h * SUB, LANES + h * SUB
+            put(RIGHT1 + first, 0, re)
+            put(RIGHT1 + first, 1, im)
+            put(RIGHT1 + second, 0, -im)
+            put(RIGHT1 + second, 1, re)
+            put(RIGHT2 + first, 0, re)
+            put(RIGHT2 + first, 1, -im)
+            put(RIGHT2 + second, 0, im)
+            put(RIGHT2 + second, 1, re)
         return carry
 
     lax.fori_loop(0, waves, one_table, 0)
-
-
-def table_call(wavelengths):
-    waves = wavelengths.shape[0]
+    for l in range(cotangent.shape[0]):
+        own = cotangent[l].astype(jnp.float32) * (2.0 / (waves * SUB))
+        slab[weight_spot(l, waves)] = jnp.concatenate([own, own], axis=1).astype(jnp.bfloat16)
+    copy = pltpu.make_async_copy(slab, slab_far.at[pl.ds(0, slab.shape[0]), :], sem)
+    copy.start()
+    copy.wait()
+
+
+def table_call(wavelengths, cotangent):
     vmem = pl.BlockSpec(memory_space=pltpu.VMEM)
+    rows = slab_rows(wavelengths.shape[0], cotangent.shape[0])
     return pl.pallas_call(
         table_kernel,
-        out_shape=[
-            jax.ShapeDtypeStruct((waves, 8, LANES), jnp.float32),
-            jax.ShapeDtypeStruct((waves, LANES, LANES), jnp.bfloat16),
-            jax.ShapeDtypeStruct((waves, LANES, LANES), jnp.bfloat16),
-            jax.ShapeDtypeStruct((waves, 2 * LANES, 2 * LANES), jnp.bfloat16),
-            jax.ShapeDtypeStruct((waves, 2 * LANES, 2 * LANES), jnp.bfloat16),
-        ],
-        in_specs=[pl.BlockSpec(memory_space=pltpu.SMEM)],
-        out_specs=[vmem] * 5,
+        out_shape=jax.ShapeDtypeStruct((max(rows, FAR_ROWS), 2 * LANES), jnp.bfloat16),
+        in_specs=[pl.BlockSpec(memory_space=pltpu.SMEM), vmem],
+        out_specs=pl.BlockSpec(memory_space=pltpu.HBM),
+        scratch_shapes=[pltpu.VMEM((rows, 2 * LANES), jnp.bfloat16), pltpu.SemaphoreType.DMA],
         compiler_params=pltpu.CompilerParams(vmem_limit_bytes=VMEM_LIMIT),
         cost_estimate=pl.CostEstimate(flops=10_000_000, bytes_accessed=6_000_000, transcendentals=0),
         name="lens_tables",
-    )(wavelengths)
-
-
-def wave_groups(group, count, owner_of, cotangent, opd, amplitude, grad, turns_per, left1, left2, right1, right2):
+    )(wavelengths, cotangent)
+
+
+def wave_groups(group, count, owner_of, opd, amplitude, grad, turns_per, slab):
     waves = turns_per.shape[0]
+    lower = lax.broadcasted_iota(jnp.int32, (SUB, LANES), 1) < SUB
 
     def stack(res, ims):
         top = jnp.concatenate([x.astype(jnp.bfloat16) for x in res], axis=1)
@@ -205,9 +220,9 @@
         totals = [None] * group
         for i in range(group):
             k = (g * group + i) * 2
-            pieces = [cotangent[owner_of[k + h]].astype(jnp.float32) for h in range(2)]
             scaled.append(amplitude[g * group + i] * LEAD**2)
-            weights.append(jnp.concatenate(pieces, axis=1) * (2.0 / (waves * SUB)))
+            pieces = [slab[weight_spot(owner_of[k + h], waves)].astype(jnp.float32) for h in range(2)]
+            weights.append(jnp.where(lower, *pieces))
 
         def field(w, state):
             scale = turns_per[w][0:1]
@@ -221,11 +236,11 @@
 
         def pupil_rows(w, state):
             reals, imags, e = state
-            return reals, imags, line(jnp.dot(left1[w], e, preferred_element_type=jnp.float32))
+            return reals, imags, line(jnp.dot(slab[pl.ds(w * WAVE_ROWS + LEFT, LANES), pl.ds(0, LANES)], e, preferred_element_type=jnp.float32))
 
         def pupil_columns(w, state):
             reals, imags, p = state
-            f = jnp.dot(p, right1[w], preferred_element_type=jnp.float32)
+            f = jnp.dot(p, slab[pl.ds(w * WAVE_ROWS + RIGHT1, 2 * LANES), :], preferred_element_type=jnp.float32)
             held = [[], []]
             for i in range(group):
                 for h in range(2):
@@ -234,11 +249,11 @@
 
         def focal_rows(w, state):
             reals, imags, held = state
-            return reals, imags, line(jnp.dot(left2[w], held, preferred_element_type=jnp.float32))
+            return reals, imags, line(jnp.dot(slab[pl.ds(w * WAVE_ROWS + LEFT, LANES), pl.ds(LANES, LANES)], held, preferred_element_type=jnp.float32))
 
         def focal_columns(w, state):
             reals, imags, q = state
-            b = jnp.dot(q, right2[w], preferred_element_type=jnp.float32)
+            b = jnp.dot(q, slab[pl.ds(w * WAVE_ROWS + RIGHT2, 2 * LANES), :], preferred_element_type=jnp.float32)
             factor = turns_per[w][0:1] * (2.0 * math.pi / SUB)
             for i in range(group):
                 back = b[SUB * i : SUB * (i + 1)]
@@ -259,24 +274,21 @@
 
 
 def wave_kernel(
-    message, cotangent, turns_far, left1_far, left2_far, right1_far, right2_far, out,
-    turns_per, left1, left2, right1, right2,
-    heads, table, place, slot_place, owner_of, opd, amplitude, grad, shades, mask, sem, table_sems,
+    lenses, waves_ref, message, slab_far, out,
+    slab, turns_per, heads, table, place, slot_place, owner_of, opd, amplitude, grad, shades, mask, sem, slab_sem,
 ):
     peers = message.shape[0]
-    lenses = cotangent.shape[0]
     pairs = opd.shape[0] - 1
     extent = mask.shape[0]
     dead_place = 2 * pairs
 
-    far = (turns_far, left1_far, right1_far, left2_far, right2_far)
-    near = (turns_per, left1, right1, left2, right2)
-    loads = [pltpu.make_async_copy(x, y, table_sems.at[i]) for i, (x, y) in enumerate(zip(far, near))]
-    for load in loads:
-        load.start()
+    load = pltpu.make_async_copy(slab_far.at[pl.ds(0, slab.shape[0]), :], slab, slab_sem)
+    load.start()
+    for w in range(waves_ref.shape[0]):
+        turns_per[w] = 1.0 / jnp.full((8, LANES), waves_ref[w], jnp.float32)
     for p in range(peers):
-        head = message[p, pl.ds(SUB, HEAD), :].astype(jnp.float32)[0:2]
-        heads[pl.ds(2 * p, 2), :] = head.astype(jnp.int32)
+        head = message[p, pl.ds(SUB, HEAD), :].astype(jnp.float32)[0:1]
+        heads[pl.ds(p, 1), :] = head.astype(jnp.int32)
     copy = pltpu.make_async_copy(heads, table, sem)
     copy.start()
     fill_mask(mask)
@@ -291,8 +303,9 @@
     copy.wait()
 
     def one_place(i, count):
-        live = table[i, 0] == 1
-        lens = table[i, 2]
+        p, c = i >> 1, i & 1
+        live = table[p, c] == 1
+        lens = table[p, 4 + c]
         before = place[lens]
         fresh = live & (before < 0)
         here = jnp.where(fresh, count, before)
@@ -307,7 +320,7 @@
         patch = message[p, pl.ds(0, SUB), :].astype(jnp.float32)
         sides = []
         for c in range(2):
-            live, row, col = (table[2 * p + c, k] for k in (0, 3, 4))
+            live, row, col = (table[p, 2 * k + c] for k in (0, 3, 4))
             sides.append(window(mask, row, col, extent, c) * live.astype(jnp.float32))
         shade = jnp.where(lower, sides[0], sides[1])
         shades[p] = shade
@@ -322,10 +335,9 @@
         return carry
 
     lax.fori_loop(0, peers, one_slot, 0, unroll=4)
-    for load in loads:
-        load.wait()
-
-    arrays = (owner_of, cotangent, opd, amplitude, grad, turns_per, left1, left2, right1, right2)
+    load.wait()
+
+    arrays = (owner_of, opd, amplitude, grad, turns_per, slab)
     few = count <= FEW
 
     @pl.when(few)
@@ -348,24 +360,29 @@
     lax.fori_loop(0, peers, one_return, 0, unroll=4)
 
 
+def all_but(size):
+    return pltpu.CompilerParams(vmem_limit_bytes=max(VMEM - size - 64 * 1024, VMEM_LIMIT))
+
+
 def round_up(value, step):
     return -(-value // step) * step
 
 
-def wave_call(tables, message, cotangent, extent):
+def wave_call(wavelengths, tables, message, lenses, extent):
     peers = message.shape[0]
-    lenses = cotangent.shape[0]
     pairs = max(round_up(lenses, 2 * GROUP), round_up(lenses, 2 * GROUP_FEW)) // 2
     vmem = pl.BlockSpec(memory_space=pltpu.VMEM)
     far = pl.BlockSpec(memory_space=pltpu.HBM)
     return pl.pallas_call(
-        wave_kernel,
+        functools.partial(wave_kernel, lenses),
         out_shape=jax.ShapeDtypeStruct((peers, SUB, LANES), jnp.bfloat16),
-        in_specs=[vmem, vmem] + [far] * len(tables),
+        in_specs=[pl.BlockSpec(memory_space=pltpu.SMEM), vmem, far],
         out_specs=vmem,
-        scratch_shapes=[pltpu.VMEM(x.shape, x.dtype) for x in tables] + [
-            pltpu.VMEM((2 * peers, LANES), jnp.int32),
-            pltpu.SMEM((2 * peers, LANES), jnp.int32),
+        scratch_shapes=[
+            pltpu.VMEM((slab_rows(wavelengths.shape[0], lenses), 2 * LANES), jnp.bfloat16),
+            pltpu.VMEM((wavelengths.shape[0], 8, LANES), jnp.float32),
+            pltpu.VMEM((peers, LANES), jnp.int32),
+            pltpu.SMEM((peers, LANES), jnp.int32),
             pltpu.SMEM((lenses,), jnp.int32),
             pltpu.SMEM((2 * peers,), jnp.int32),
             pltpu.SMEM((2 * pairs + 1,), jnp.int32),
@@ -375,11 +392,11 @@
             pltpu.VMEM((peers, SUB, LANES), jnp.float32),
             pltpu.VMEM((extent, extent), jnp.float32),
             pltpu.SemaphoreType.DMA,
-            pltpu.SemaphoreType.DMA((len(tables),)),
+            pltpu.SemaphoreType.DMA,
         ],
         compiler_params=pltpu.CompilerParams(vmem_limit_bytes=VMEM_LIMIT),
         name="wave_gradients",
-    )(message, cotangent, *tables)
+    )(wavelengths, message, tables)
 
 
 def place_kernel(entries, patches, out, heads, table, sem):
@@ -394,7 +411,7 @@
     def one_peer(p, carry):
         both = jnp.concatenate([patches[p].astype(jnp.float32), spare], axis=0)
         for c in range(2):
-            seg, row, col = (table[2 * p + c, k] for k in (1, 3, 4))
+            seg, row, col = (table[2 * k + c, p] for k in (1, 3, 4))
             base, down = aligned(row, extent)
             moved = pltpu.roll(both, (col + LANES - SUB * c) & (LANES - 1), axis=1)
             moved = pltpu.roll(moved, down, axis=0)
@@ -412,27 +429,30 @@
     peers = intersections.shape[0]
     segs, extent, _ = segment_maps.shape
     vmem = pl.BlockSpec(memory_space=pltpu.VMEM)
-    table_space = [pltpu.VMEM((2 * peers, LANES), jnp.int32), pltpu.SMEM((2 * peers, LANES), jnp.int32)]
+    entries = jnp.transpose(intersections, (2, 1, 0))
+    table_shape = (HEAD_ROWS, round_up(peers, LANES))
+    table_space = [pltpu.VMEM(table_shape, jnp.int32), pltpu.SMEM(table_shape, jnp.int32)]
     params = pltpu.CompilerParams(vmem_limit_bytes=VMEM_LIMIT)
 
     message = pl.pallas_call(
         cut_kernel,
         out_shape=jax.ShapeDtypeStruct((peers, SUB + HEAD, LANES), jnp.bfloat16),
-        in_specs=[vmem, pl.BlockSpec(memory_space=pltpu.HBM)],
+        in_specs=[pl.BlockSpec(memory_space=pl.ANY)] * 2,
         out_specs=vmem,
         scratch_shapes=[
+            pltpu.VMEM(entries.shape, jnp.int32),
             *table_space,
             pltpu.VMEM((segs, extent, extent), jnp.bfloat16),
             pltpu.VMEM((segs, extent, extent), jnp.float32),
             pltpu.SemaphoreType.DMA,
             pltpu.SemaphoreType.DMA((segs,)),
         ],
-        compiler_params=params,
+        compiler_params=all_but(peers * (SUB + HEAD) * LANES * 2),
         name="cut_patches",
-    )(intersections, segment_maps)
-    tables = table_call(wavelengths)
+    )(entries, segment_maps)
+    tables = table_call(wavelengths, cotangent)
     arriving = lax.all_to_all(message, "tile", split_axis=0, concat_axis=0, tiled=True)
-    grads = wave_call(tables, arriving, cotangent, extent)
+    grads = wave_call(wavelengths, tables, arriving, cotangent.shape[0], extent)
     returned = lax.all_to_all(grads, "tile", split_axis=0, concat_axis=0, tiled=True)
     return pl.pallas_call(
         place_kernel,
@@ -442,7 +462,7 @@
         scratch_shapes=[*table_space, pltpu.SemaphoreType.DMA],
         compiler_params=params,
         name="place_gradients",
-    )(intersections, returned)
+    )(entries, returned)
 
 
 def solution(mesh):

time: 50.2 us -> 47.2 us (0.940)
  Pallas kernels: 14 us -> 17.4 us
  local copies, waits for them, and re-layouts: 4.81 us -> 1.65 us
  waiting for transfers between devices: 6.79 us -> 4.21 us
  blocking collectives: 16.9 us -> 16.1 us
    pallas_call x2, Pallas kernels: 8.63 us -> 12 us  [the longest x1 7.34 us: wave_call(): pl.pallas_call(functools.partial(wave_kernel, lenses), out_shape=jax.Shap...]
    unnamed x9 -> x8, local copies, waits for them, and re-layouts: 4.81 us -> 1.65 us
    all_to_all x1, waiting for transfers between devices: 6.79 us -> 4.21 us  [on_device(): lax.all_to_all(message, 'tile', split_axis=0, concat_axis=0, tiled=True)]
    all_to_all x1, blocking collectives: 16.9 us -> 16.1 us  [on_device(): lax.all_to_all(grads, 'tile', split_axis=0, concat_axis=0, tiled=True)]
  transfers between devices with their start and end apart: 1 -> 1, of which waited for: 1 -> 1; matrix products, arithmetic and copies ran while one was open for 0% -> 0% of each run, Pallas kernels for 4% -> 10%
where the time goes in v4:
time: 47.2 us; the launch traced here: 46.8 us
  Pallas kernels  17.4 us (37%)
  blocking collectives  16.1 us (34%)
  starting transfers between devices  7.4 us (16%)
  waiting for transfers between devices  4.21 us (9%)
  local copies, waits for them, and re-layouts  1.65 us (3%)
    all_to_all x1, blocking collectives, on_device(): lax.all_to_all(grads, 'tile', split_axis=0, concat_axis=0, tiled=True)  16.1 us
    all_to_all x1, starting transfers between devices, on_device(): lax.all_to_all(message, 'tile', split_axis=0, concat_axis=0, tiled=True)  7.4 us
    pallas_call x1, Pallas kernels, wave_call(): pl.pallas_call(functools.partial(wave_kernel, lenses), out_shape=jax.Shap...  7.34 us
    pallas_call x1, Pallas kernels, table_call(): pl.pallas_call(table_kernel, out_shape=jax.ShapeDtypeStruct((max(rows, FA...  4.69 us
    all_to_all x1, waiting for transfers between devices, on_device(): lax.all_to_all(message, 'tile', split_axis=0, concat_axis=0, tiled=True)  4.21 us
    pallas_call x1, Pallas kernels, on_device(): pl.pallas_call(cut_kernel, out_shape=jax.ShapeDtypeStruct((peers, SUB + H...  2.93 us
    pallas_call x1, Pallas kernels, on_device(): pl.pallas_call(place_kernel, out_shape=jax.ShapeDtypeStruct((segs, extent...  2.43 us
    unnamed x8, local copies, waits for them, and re-layouts  1.65 us
  transfers between devices with their start and end apart: 1, of which 1 were waited for; matrix products, arithmetic and copies ran while one was open for 0% of the time, Pallas kernels for 10%

profile of v4, /device:TPU:0, one launch (start us, length us, event | category | flops | bytes accessed | tf_op | source)
XLA Modules:
  0.0 46.8 jit_solution(5444236412832527956)
XLA Ops:
  0.0 0.0 copy-start.3
  0.0 2.9 %cut_patches.1 = bf16[16,72,128]{2,1,0:T(8,128)(2,1)} custom-call(s32[5,2,16]{2,1,0:T(2,128)} %bitcast.1, bf16[4,256,256]{2,1,0:T(8,128)(2,1)} %maps.1), custom_call_target="tpu_custom_call" | custom-call | tf_op jit(solution)/shard_map/cut_patches/pallas_call | solution.py:437
  2.9 7.4 %all-to-all-start = ((bf16[16,72,128]{2,1,0:T(8,128)(2,1)}), bf16[16,72,128]{2,1,0:T(8,128)(2,1)S(1)}, u32[]{:S(2)}, u32[]{:S(2)}) async-start(bf16[16,72,128]{2,1,0:T(8,128)(2,1)} %cut_patches.1), calls=%async_computation | async-start | bytes 589824 | tf_op jit(solution)/shard_map/all_to_all | solution.py:454
  10.3 0.0 copy-start
  10.4 1.0 %copy-done = bf16[24,64,64]{2,1,0:T(8,128)(2,1)S(1)} copy-done((bf16[24,64,64]{2,1,0:T(8,128)(2,1)S(1)}, bf16[24,64,64]{2,1,0:T(8,128)(2,1)}, u32[]{:S(2)}) %copy-start) | copy-done | bytes 196632
  11.3 0.0 copy-start.2
  11.3 0.7 %copy-done.2 = f32[16]{0:T(128)S(1)} copy-done((f32[16]{0:T(128)S(1)}, f32[16]{0:T(128)}, u32[]{:S(2)}) %copy-start.2) | copy-done | bytes 88
  12.0 0.0 copy-start.1
  12.0 4.7 %lens_tables.1.slab_far = bf16[40960,256]{1,0:T(8,128)(2,1)} custom-call(f32[16]{0:T(128)S(1)} %copy-done.2, bf16[24,64,64]{2,1,0:T(8,128)(2,1)S(1)} %copy-done), custom_call_target="tpu_custom_call" | custom-call | flops 10000000 | bytes 6000000 | tf_op jit(solution)/shard_map/lens_tables/pallas_call | solution.py:189
  16.7 4.2 %all-to-all-done.message = bf16[16,72,128]{2,1,0:T(8,128)(2,1)S(1)} async-done(((bf16[16,72,128]{2,1,0:T(8,128)(2,1)}), bf16[16,72,128]{2,1,0:T(8,128)(2,1)S(1)}, u32[]{:S(2)}, u32[]{:S(2)}) %all-to-all-start) | async-done | bytes 294944 | tf_op jit(solution)/shard_map/all_to_all | solution.py:454
  20.9 0.0 copy-done.3
  20.9 7.3 %wave_gradients.1 = bf16[16,64,128]{2,1,0:T(8,128)(2,1)S(1)} custom-call(f32[16]{0:T(128)S(1)} %copy-done.3, bf16[16,72,128]{2,1,0:T(8,128)(2,1)S(1)} %all-to-all-done.message, bf16[40960,256]{1,0:T(8,128)(2,1)} %lens_tables.1.slab_far), custom_call_target="tpu_custom_call" | custom-call | tf_op jit(solution)/shard_map/wave_gradients/pallas_call | solution.py:376
  28.3 16.1 %all_to_all.10.patches = bf16[16,64,128]{2,1,0:T(8,128)(2,1)S(1)} all-to-all(bf16[16,64,128]{2,1,0:T(8,128)(2,1)S(1)} %wave_gradients.1), channel_id=1, replica_groups=mesh['case'=2,'tile'=16] {'tile'}, dimensions={0} | all-to-all | bytes 524288 | tf_op jit(solution)/shard_map/all_to_all | solution.py:456
  44.3 0.0 copy-done.1
  44.3 2.4 %place_gradients.1 = f32[4,256,256]{2,1,0:T(8,128)} custom-call(s32[5,2,16]{2,1,0:T(2,128)S(1)} %bitcast.2, bf16[16,64,128]{2,1,0:T(8,128)(2,1)S(1)} %all_to_all.10.patches), custom_call_target="tpu_custom_call" | custom-call | tf_op jit(solution)/shard_map/place_gradients/pallas_call | solution.py:457
Async XLA Ops:
  0.0 20.9 %copy-start.3 = (f32[16]{0:T(128)S(1)}, f32[16]{0:T(128)}, u32[]{:S(2)}) copy-start(f32[16]{0:T(128)} %waves_ref.3) | copy-start | bytes 196
  2.9 18.0 %all-to-all-start = ((bf16[16,72,128]{2,1,0:T(8,128)(2,1)}), bf16[16,72,128]{2,1,0:T(8,128)(2,1)S(1)}, u32[]{:S(2)}, u32[]{:S(2)}) async-start(bf16[16,72,128]{2,1,0:T(8,128)(2,1)} %cut_patches.1), calls=%async_computation | async-start | bytes 589824 | tf_op jit(solution)/shard_map/all_to_all | solution.py:454
  10.3 1.0 %copy-start = (bf16[24,64,64]{2,1,0:T(8,128)(2,1)S(1)}, bf16[24,64,64]{2,1,0:T(8,128)(2,1)}, u32[]{:S(2)}) copy-start(bf16[24,64,64]{2,1,0:T(8,128)(2,1)} %cotangent.1) | copy-start | bytes 589828
  11.3 0.7 %copy-start.2 = (f32[16]{0:T(128)S(1)}, f32[16]{0:T(128)}, u32[]{:S(2)}) copy-start(f32[16]{0:T(128)} %waves_ref.3) | copy-start | bytes 196
  12.0 32.3 %copy-start.1 = (s32[16,2,5]{0,1,2:T(2,128)S(1)}, s32[16,2,5]{0,1,2:T(2,128)}, u32[]{:S(2)}) copy-start(s32[16,2,5]{0,1,2:T(2,128)} %param.7) | copy-start | bytes 1924
